TPU v7x, 512 devices: a whole 4x4x16 slice. The times are simulated.
512 devices in a mesh: wide: 128 (over y, z, core), head: 4 (over x).
Axes of the slice: x: 4, y: 4, z: 16, core: 2. Of those that a mesh axis runs over, the one named last changes fastest.
Arguments:
- hidden_in: bfloat16 [16384, 4096], P('wide', 'head'), may hold values from -6 to 6
- enc_query: bfloat16 [16384, 2048], P('wide', 'head'), may hold values from -160 to 160
- enc_key: bfloat16 [16384, 2048], P('wide', 'head'), may hold values from -6 to 6
- enc_value: bfloat16 [16384, 2048], P('wide', 'head'), may hold values from -6 to 6
- dec_query: bfloat16 [8192, 2048], P('wide', 'head'), may hold values from -6 to 6
- out_proj: bfloat16 [2048, 4096], P('head', 'wide'), may hold values from -0.125 to 0.125
- key_proj: bfloat16 [4096, 2048], P('wide', 'head'), may hold values from -0.09375 to 0.09375
- value_proj: bfloat16 [4096, 2048], P('wide', 'head'), may hold values from -0.09375 to 0.09375
- norm_gain: float32 [4096], replicated, may hold values from 0.25 to 1.75
- enc_len: int32 [256], replicated, may hold values from 33 to 128, as said below
- dec_len: int32 [256], replicated, may hold values from 17 to 64, as said below
- example_order: int32 [256], replicated, may hold values from 0 to 255, as said below
- enc_bounds: int32 [129], replicated, may hold values from 0 to 256, as said below
- dec_bounds: int32 [129], replicated, may hold values from 0 to 256, as said below
Outputs:
- encoder_hidden: bfloat16 [16384, 4096], P('wide', 'head')
- cross_context: bfloat16 [8192, 2048], P('wide', 'head')
Inputs may be any that keep to these rules, and one draw needn't show every extreme that they name: `enc_len`: the examples of one wide device in the encoder layout fill at most 128 rows; the last device holds one example of exactly 128 rows. `dec_len`: the examples of one wide device in the decoder layout fill at most 64 rows; the first device holds one example of exactly 64 rows. `example_order`: A permutation of the examples. `enc_bounds`: nondecreasing from 0 to 256; every device gets one to three examples. `dec_bounds`: nondecreasing from 0 to 256; every device gets one to three examples; one less than enc_bounds at every inner index.
All inputs are finite; a program needn't handle non-finite values.
Results may differ from a plain program's by a relative error of at most 0.0073.
Values may be sent and summed in bfloat16 or wider, within the bound.
A program may use at most 64 MiB of HBM per device.

v0:
```python
import math

import jax
import jax.numpy as jnp
from jax import lax
from jax.sharding import PartitionSpec as P

HEAD_DIM = 256


epsilon = 1e-06


def passed_along(value, axis, steps):
    count = lax.axis_size(axis)
    initial, last = (max(0, -steps), min(count, count - steps))
    return lax.ppermute(value, axis, [(source, source + steps) for source in range(initial, last)])


def row_tags(lengths, example_order, bounds, device, row_count):
    example_count = example_order.shape[0]
    places = jnp.arange(example_count, dtype=jnp.int32)
    picked = (example_order[:, None] == places[None, :]).astype(jnp.int32)
    sorted_len = jnp.sum(picked * lengths[None, :], axis=1)
    end_rows = jnp.cumsum(sorted_len)
    start_rows = end_rows - sorted_len
    edge_index = jnp.arange(bounds.shape[0], dtype=jnp.int32)
    first_pos = jnp.sum(jnp.where(edge_index == device, bounds, 0))
    last_pos = jnp.sum(jnp.where(edge_index == device + 1, bounds, 0))
    row_base = jnp.sum(jnp.where(places == first_pos, start_rows, 0))
    offsets = row_base + jnp.arange(row_count, dtype=jnp.int32)
    position = jnp.sum((end_rows[None, :] <= offsets[:, None]).astype(jnp.int32), axis=1)
    inside = (position < last_pos) & (device >= 0) & (device < bounds.shape[0] - 1)
    return jnp.where(inside, position, -1)


def attend(queries, key_rows, value_rows, query_tags, key_tags):
    query_count = queries.shape[0]
    heads_here = queries.shape[1] // HEAD_DIM
    query_heads = queries.reshape(query_count, heads_here, HEAD_DIM)
    key_heads = key_rows.reshape(key_rows.shape[0], heads_here, HEAD_DIM)
    value_heads = value_rows.reshape(value_rows.shape[0], heads_here, HEAD_DIM)
    scores = jnp.einsum("qhd,khd->hqk", query_heads, key_heads, preferred_element_type=jnp.float32)
    scores = scores * (1.0 / math.sqrt(HEAD_DIM))
    matched = (query_tags[:, None] == key_tags[None, :]) & (key_tags[None, :] >= 0)
    scores = jnp.where(matched[None], scores, -1e30)
    row_max = jnp.max(scores, axis=2, keepdims=True)
    weights = jnp.exp(scores - row_max) * matched[None].astype(jnp.float32)
    denominator = jnp.maximum(jnp.sum(weights, axis=2, keepdims=True), 1.0)
    shares = (weights / denominator).astype(jnp.bfloat16)
    context = jnp.einsum("hqk,khd->qhd", shares, value_heads, preferred_element_type=jnp.float32)
    return context.reshape(query_count, -1).astype(jnp.bfloat16)


def body(
    hidden_in,
    enc_query,
    enc_key,
    enc_value,
    dec_query,
    out_proj,
    key_proj,
    value_proj,
    norm_gain,
    enc_len,
    dec_len,
    example_order,
    enc_bounds,
    dec_bounds,
):
    device = lax.axis_index("wide")
    enc_rows = enc_query.shape[0]
    dec_rows = dec_query.shape[0]
    enc_tags = row_tags(enc_len, example_order, enc_bounds, device, enc_rows)
    context = attend(enc_query, enc_key, enc_value, enc_tags, enc_tags)
    gathered = jnp.dot(
        context,
        lax.all_gather(out_proj, "wide", axis=1, tiled=True),
        preferred_element_type=jnp.float32,
    )
    slice_cols = hidden_in.shape[1]
    column_start = lax.axis_index("head") * slice_cols
    total_sum = lax.psum(gathered, "head")
    full_rows = lax.all_gather(hidden_in, "head", axis=1, tiled=True)
    residual = full_rows.astype(jnp.float32) + total_sum
    mean_square = jnp.mean(residual * residual, axis=1, keepdims=True)
    normed = (residual * lax.rsqrt(mean_square + epsilon) * norm_gain[None, :]).astype(jnp.bfloat16)
    encoder_hidden = lax.dynamic_slice_in_dim(residual, column_start, slice_cols, 1).astype(
        jnp.bfloat16
    )
    key_sum = jnp.dot(
        normed,
        lax.all_gather(key_proj, "wide", axis=0, tiled=True),
        preferred_element_type=jnp.float32,
    )
    value_sum = jnp.dot(
        normed,
        lax.all_gather(value_proj, "wide", axis=0, tiled=True),
        preferred_element_type=jnp.float32,
    )
    cross_keys = key_sum.astype(jnp.bfloat16)
    cross_values = value_sum.astype(jnp.bfloat16)
    dec_tags = row_tags(dec_len, example_order, dec_bounds, device, dec_rows)
    lower_keys, lower_values = passed_along((cross_keys, cross_values), "wide", 1)
    near_keys = jnp.concatenate([lower_keys, cross_keys], axis=0)
    near_values = jnp.concatenate([lower_values, cross_values], axis=0)
    near_tags = jnp.concatenate(
        [row_tags(enc_len, example_order, enc_bounds, device - 1, enc_rows), enc_tags], axis=0
    )
    cross_context = attend(dec_query, near_keys, near_values, dec_tags, near_tags)
    return (encoder_hidden, cross_context)


def solution(mesh):
    return jax.shard_map(
        body,
        mesh=mesh,
        in_specs=(
            P("wide", "head"),
            P("wide", "head"),
            P("wide", "head"),
            P("wide", "head"),
            P("wide", "head"),
            P("head", "wide"),
            P("wide", "head"),
            P("wide", "head"),
            P(),
            P(),
            P(),
            P(),
            P(),
            P(),
        ),
        out_specs=(P("wide", "head"), P("wide", "head")),
        check_vma=False,
    )
```

profile of v0, /device:TPU:1, one launch (start us, length us, event | category | flops | bytes accessed | tf_op | source)
XLA Modules:
  0.0 567.7 jit_solution(6170566730653007631)
XLA Ops:
  7.2 0.7 all-gather.7.cloned.1.call-update
  7.9 0.7 all-gather.5.cloned.1.call-update
  8.7 0.9 select_reduce_fusion
  9.6 0.3 reduce-window.16
  10.2 1.4 fusion.27
  11.6 2.1 fusion.30
  13.6 0.6 iota_add_fusion
  14.3 0.7 iota_add_fusion.2
  15.1 0.6 broadcast_compare_fusion.1
  15.9 1.2 fusion.11
  17.1 1.2 fusion.4
  18.4 140.5 %all-gather.7.cloned.1.call-done = bf16[512,4096]{0,1:T(8,128)(2,1)} async-done(((bf16[512,32]{0,1:T(8,128)(2,1)}), bf16[512,4096]{0,1:T(8,128)(2,1)}) %all-gather.7.cloned.1.call-update) | async-done | bytes 4194320 | tf_op jit(solution)/shard_map/all_gather | solution.py:78
  159.0 5.0 fusion.40
  164.0 0.5 all-gather.11.cloned.1.call-update
  164.6 0.5 all-gather.9.cloned.1.call-update
  165.5 0.7 and_select_fusion
  166.3 1.3 fusion.29
  167.6 0.6 iota_add_fusion.1
  168.5 0.6 and_select_fusion.1
  169.1 18.1 %all-gather.5.cloned.1.call-done = bf16[128,4096]{1,0:T(8,128)(2,1)} async-done(((bf16[128,1024]{1,0:T(8,128)(2,1)}), bf16[128,4096]{1,0:T(8,128)(2,1)}) %all-gather.5.cloned.1.call-update) | async-done | bytes 1048592 | tf_op jit(solution)/shard_map/all_gather | solution.py:84
  187.3 77.8 %all-reduce.2.cloned.1.call-done = f32[128,4096]{1,0:T(8,128)} async-done(((f32[128,4096]{1,0:T(8,128)}), f32[128,4096]{1,0:T(8,128)}) %all-reduce.2.cloned.1.call-update) | async-done | bytes 2097168 | tf_op jit(solution)/shard_map/psum | solution.py:83
  265.0 2.2 multiply_reduce_fusion
  267.3 143.5 %all-gather.11.cloned.1.call-done = bf16[4096,512]{1,0:T(8,128)(2,1)} async-done(((bf16[32,512]{1,0:T(8,128)(2,1)}), bf16[4096,512]{1,0:T(8,128)(2,1)}) %all-gather.11.cloned.1.call-update) | async-done | bytes 4194320 | tf_op jit(solution)/shard_map/all_gather | solution.py:93
  410.8 2.9 convolution_convert_fusion
  413.8 3.2 collective-permute-start.1
  417.0 135.2 %all-gather.9.cloned.1.call-done = bf16[4096,512]{1,0:T(8,128)(2,1)} async-done(((bf16[32,512]{1,0:T(8,128)(2,1)}), bf16[4096,512]{1,0:T(8,128)(2,1)}) %all-gather.9.cloned.1.call-update) | async-done | bytes 4194320 | tf_op jit(solution)/shard_map/all_gather | solution.py:98
  552.3 2.9 convolution_convert_fusion.1
  555.2 3.1 collective-permute-start
  558.3 0.7 dynamic-slice_convert_fusion
  559.1 0.4 fusion.35
  559.5 0.8 collective-permute-done
  560.5 0.6 copy.48
  (32 shorter events, 2.0 us)
Async XLA Ops:
  7.2 151.8 %all-gather.7.cloned.1.call-start = ((), (), s32[]{:S(2)}) async-start(), calls=%async_computation.1 | async-start | bytes 4227072 | tf_op jit(solution)/shard_map/all_gather | solution.py:78
  7.9 179.4 %all-gather.5.cloned.1.call-start = ((), (), s32[]{:S(2)}) async-start(), calls=%async_computation | async-start | bytes 1310720 | tf_op jit(solution)/shard_map/all_gather | solution.py:84
  8.6 256.4 %all-reduce.2.cloned.1.call-start = ((), (), s32[]{:S(2)}) async-start(), calls=%async_computation.2 | async-start | bytes 4194304 | tf_op jit(solution)/shard_map/psum | solution.py:83
  164.0 246.9 %all-gather.11.cloned.1.call-start = ((), (), s32[]{:S(2)}) async-start(), calls=%async_computation.4 | async-start | bytes 4227072 | tf_op jit(solution)/shard_map/all_gather | solution.py:93
  164.5 387.8 %all-gather.9.cloned.1.call-start = ((), (), s32[]{:S(2)}) async-start(), calls=%async_computation.3 | async-start | bytes 4227072 | tf_op jit(solution)/shard_map/all_gather | solution.py:98
  169.1 241.7 %copy-start = (f32[4096]{0:T(1024)S(1)}, f32[4096]{0:T(1024)}, u32[]{:S(2)}) copy-start(f32[4096]{0:T(1024)} %param.22) | copy-start | bytes 49156
  413.8 145.3 %copy-start.1 = (bf16[64,512]{1,0:T(8,128)(2,1)S(1)}, bf16[64,512]{1,0:T(8,128)(2,1)}, u32[]{:S(2)}) copy-start(bf16[64,512]{1,0:T(8,128)(2,1)} %param.18) | copy-start | bytes 196612
  413.8 145.3 %collective-permute-start.1 = (bf16[128,512]{1,0:T(8,128)(2,1)S(1)}, bf16[128,512]{1,0:T(8,128)(2,1)S(1)}, u32[]{:S(2)}, u32[]{:S(2)}) collective-permute-start(bf16[128,512]{1,0:T(8,128)(2,1)S(1)} %convolution_convert_fusion), channel_id=1, source_target_pairs={{0,4},{4,8},{8,12},{12,16},{16,20},{20,24},{24,28},{28,32},{32,36}... | collective-permute-start | bytes 393224 | tf_op jit(solution)/shard_map/ppermute | solution.py:17
  555.2 5.0 collective-permute-start
Sparse Core Ops, SparseCore 0:
  11.1 147.7 all-gather.6
  161.1 26.1 all-gather.4
  189.6 75.3 all-reduce.1
  268.5 142.2 all-gather.10
  414.3 137.9 all-gather.8
where the time goes:
time: 569 us; the launch traced here: 568 us
  waiting for transfers between devices  518 us (91%)
  between operations  14 us (2%)
  matrix products  13.8 us (2%)
  other arithmetic  13.1 us (2%)
  starting transfers between devices  6.49 us (1%)
    all_gather x1, waiting for transfers between devices, body(): lax.all_gather(key_proj, 'wide', axis=0, tiled=True)  144 us
    all_gather x1, waiting for transfers between devices, body(): lax.all_gather(out_proj, 'wide', axis=1, tiled=True)  141 us
    all_gather x1, waiting for transfers between devices, body(): lax.all_gather(value_proj, 'wide', axis=0, tiled=True)  135 us
    psum x1, waiting for transfers between devices, body(): total_sum = lax.psum(gathered, 'head')  77.8 us
    all_gather x1, waiting for transfers between devices, body(): full_rows = lax.all_gather(hidden_in, 'head', axis=1, tiled=True)  18.1 us
  transfers between devices with their start and end apart: 7, of which 6 were waited for; matrix products, arithmetic and copies ran while one was open for 5% of the time, Pallas kernels for 0%

commit v1 on v0

v1 whole, which is shorter than its diff:
```python
import jax
import jax.numpy as jnp
from jax import lax
from jax.experimental import pallas as pl
from jax.experimental.pallas import tpu as pltpu
from jax.sharding import PartitionSpec as P

MESH = pl.DeviceIdType.MESH
F32 = jnp.float32
BF16 = jnp.bfloat16

HEAD_DIM = 256
NZ = 16
NY = 4
NX = 4
NW = NY * NZ * 2
ROWS = 128
DROWS = 64
WID = 512
PIECE = 32
BLK = 2 * PIECE
FEAT = NZ * BLK
STEPS = NZ // 2
GROUP = NY * ROWS
EPSILON = 1e-06
SCALE = 1.0 / 16.0
VMEM_LIMIT = 60 * 1024 * 1024


def nt(a, b):
    return lax.dot_general(a, b, (((1,), (1,)), ((), ())), preferred_element_type=F32)


def nn(a, b):
    return lax.dot_general(a, b, (((1,), (0,)), ((), ())), preferred_element_type=F32)


def iota(shape, dim):
    return lax.broadcasted_iota(jnp.int32, shape, dim)


def attend(q, k, v, allowed):
    scores = jnp.where(allowed, nt(q, k) * SCALE, -1e30)
    weights = jnp.where(allowed, jnp.exp(scores - jnp.max(scores, axis=1, keepdims=True)), 0.0)
    total = jnp.maximum(jnp.sum(weights, axis=1, keepdims=True), 1.0)
    return nn((weights / total).astype(BF16), v).astype(BF16)


def kernel(
    hidden, q_hbm, k_hbm, v_hbm, dq_hbm, wo_hbm, wk_hbm, wv_hbm, gain_hbm,
    elen_hbm, dlen_hbm, order_hbm, ebound_hbm, dbound_hbm,
    enc_out, cross_out,
    q_ref, k_ref, v_ref, gain_ref, gain_col, lens_ref, ebound, dbound,
    wo, kvw, ctx, hid, hid_t, hid_c, hid_in, part, x1s, x1r, x2s, x2r, res_t, acc, sums, out_t, out_c, out_in,
    ys, yr, ss_s, ss_r, dq2, dres, drecv,
    in_sem, sib_s, sib_r, wo_s, wo_r, wof_s, wof_r, key_s, key_r, keyf_s, keyf_r,
    val_s, val_r, valf_s, valf_r, misc_s, misc_r, hid_s, hid_r, out_s, out_r, ctx_s, ctx_r, xs1, xr1, xs2, xr2, y_s, y_r, st_s, st_r,
):
    w = lax.axis_index("wide")
    x = lax.axis_index("head")
    c = w % 2
    z = (w // 2) % NZ
    y = w // (2 * NZ)
    step_dir = 1 - 2 * c

    def wide(yy, zz, cc):
        return (yy * NZ + zz) * 2 + cc

    sib = (w + step_dir, x)
    z_next = (wide(y, (z + step_dir + NZ) % NZ, c), x)
    z_prev = (wide(y, (z - step_dir + NZ) % NZ, c), x)
    ya, yb, y2 = y + 1 - 2 * (y % 2), NY - 1 - y, (y + 2) % NY
    y_a, y_b, y_2 = (wide(ya, z, c), x), (wide(yb, z, c), x), (wide(y2, z, c), x)
    x_a, x_b = (w, x + 1 - 2 * (x % 2)), (w, NX - 1 - x)
    upper, lower = ((w + 1) % NW, x), ((w + NW - 1) % NW, x)
    adder = (wide(x, z, c), x)
    off_diagonal = x != y
    greet = (sib, z_next, z_prev, y_a, y_b, y_2, x_a, x_b, upper, lower)

    def remote(src, dst, ss, rs, dev):
        return pltpu.make_async_remote_copy(
            src_ref=src, dst_ref=dst, send_sem=ss, recv_sem=rs, device_id=dev, device_id_type=MESH
        )

    barrier = pltpu.get_barrier_semaphore()
    for dev in greet:
        pl.semaphore_signal(barrier, inc=1, device_id=dev, device_id_type=MESH)

    mine = pl.ds(pl.multiple_of(z * BLK + c * PIECE, PIECE), PIECE)
    pairs = (
        (wo_hbm, wo.at[mine]), (elen_hbm, lens_ref.at[0]), (dlen_hbm, lens_ref.at[1]),
        (order_hbm, lens_ref.at[2]), (ebound_hbm, ebound), (dbound_hbm, dbound),
        (q_hbm, q_ref), (k_hbm, k_ref), (v_hbm, v_ref),
        (wk_hbm, kvw.at[0, mine]), (wv_hbm, kvw.at[1, mine]), (hidden, hid),
        (gain_hbm, gain_ref), (dq_hbm, dq2.at[pl.ds(0, DROWS)]),
    )
    loads = [pltpu.make_async_copy(a, b, in_sem.at[i]) for i, (a, b) in enumerate(pairs)]
    for load in loads:
        load.start()
    for load in loads[:6]:
        load.wait()

    n = 256
    onehot = jnp.where(lens_ref[2] == iota((n, n), 0), 1.0, 0.0).astype(BF16)
    lens = jnp.concatenate([lens_ref[0], lens_ref[1], jnp.zeros((6, n), jnp.int32)], axis=0)
    ordered = nn(lens.astype(F32).astype(BF16), onehot)
    upto = jnp.where(iota((n, n), 0) <= iota((n, n), 1), 1.0, 0.0).astype(BF16)
    ends = nn(ordered.astype(BF16), upto)
    place = iota((1, n), 1)

    def start(row, first):
        return jnp.sum(jnp.where(place < first, row, 0.0), axis=1, keepdims=True)

    def tags(ends_row, offsets, last):
        pos = jnp.sum(jnp.where(ends_row <= offsets, 1.0, 0.0), axis=1, keepdims=True)
        return jnp.where(pos < last, pos, -1.0)

    rows_i = iota((ROWS, 1), 0)
    enc_base = start(ordered[0:1], ebound[w])
    enc_col = tags(ends[0:1], enc_base + rows_i.astype(F32), ebound[w + 1].astype(F32))
    diag = iota((ROWS, ROWS), 0) == iota((ROWS, ROWS), 1)
    enc_row = jnp.sum(jnp.where(diag, enc_col, 0.0), axis=0, keepdims=True)
    enc_allowed = (enc_col == enc_row) & (enc_row >= 0.0)

    pl.semaphore_wait(barrier, len(greet))

    sib_wo = remote(wo.at[mine], wo.at[mine], sib_s.at[0], sib_r.at[0], sib)
    sib_wo.start()
    for load in loads[6:]:
        load.wait()
    sib_kv = remote(kvw.at[:, mine], kvw.at[:, mine], sib_s.at[1], sib_r.at[1], sib)
    sib_kv.start()
    dq_copy = remote(dq_hbm, dq2.at[pl.ds(DROWS, DROWS)], misc_s.at[1], misc_r.at[1], lower)
    dq_copy.start()

    def block(i):
        return pl.ds(pl.multiple_of(((i + NZ) % NZ) * BLK, BLK), BLK)

    def hop(i, buffer, ss, rs):
        at = buffer(z - step_dir * (i - 1))
        return remote(at, at, ss.at[i - 1], rs.at[i - 1], z_next)

    def got(i, buffer, ss, rs):
        at = buffer(z - step_dir * i)
        return remote(at, at, ss.at[i - 1], rs.at[i - 1], z_next)

    def fan(i, buffer, ss, rs):
        at = buffer(z - step_dir * i)
        return remote(at, at, ss.at[i - 1], rs.at[i - 1], sib)

    def fan_got(i, buffer, ss, rs):
        at = buffer(z + step_dir * i)
        return remote(at, at, ss.at[i - 1], rs.at[i - 1], sib)

    ring_wo = (lambda i: wo.at[block(i)], wo_s, wo_r)
    ring_key = (lambda i: kvw.at[0, block(i)], key_s, key_r)
    ring_val = (lambda i: kvw.at[1, block(i)], val_s, val_r)
    fan_wo = (ring_wo[0], wof_s, wof_r)
    fan_key = (ring_key[0], keyf_s, keyf_r)
    fan_val = (ring_val[0], valf_s, valf_r)

    def pass_on(i, ring, side):
        got(i, *ring).wait_recv()

        @pl.when(i < STEPS)
        def _():
            hop(i + 1, *ring).start()
            fan(i, *side).start()

    def pair(h):
        low = jnp.where(h == STEPS, z, z - h)
        return low, z + h

    def round_one(h):
        return [
            remote(
                x1s.at[h - 1, pl.ds(half * BLK, BLK)], x1r.at[h - 1, pl.ds(half * BLK, BLK)],
                xs1.at[h - 1, half], xr1.at[h - 1, half], (x_a, x_b)[half],
            )
            for half in range(2)
        ]

    def round_two(h):
        return [
            remote(
                x2s.at[h - 1, pl.ds(half * BLK, BLK)], x2r.at[h - 1, pl.ds(half * BLK, BLK)],
                xs2.at[h - 1, half], xr2.at[h - 1, half], (x_b, x_a)[half],
            )
            for half in range(2)
        ]

    away = (y - x + NY) % NY

    def hid_copy(h):
        at = jnp.maximum(away, 1) - 1
        return remote(hid_c.at[h - 1], hid_in.at[h - 1, y], hid_s.at[h - 1], hid_r.at[h - 1, at], adder)

    def hid_got(h, d):
        at = hid_in.at[h - 1, (y + d) % NY]
        return remote(at, at, hid_s.at[h - 1], hid_r.at[h - 1, d - 1], adder)

    def out_copy(h, d):
        g = (y + d) % NY
        return remote(
            out_c.at[h - 1, g], out_in.at[h - 1], out_s.at[h - 1, d - 1], out_r.at[h - 1],
            (wide(g, z, c), x),
        )

    sib_wo.wait_recv()
    hop(1, *ring_wo).start()

    def ctx_copy(head, slot, index, dev):
        at = ctx.at[head, slot]
        return remote(at, at, ctx_s.at[index], ctx_r.at[index], dev)

    ctx_sent = []
    for head in range(2):
        cols = slice(head * HEAD_DIM, (head + 1) * HEAD_DIM)
        ctx[head, y] = attend(q_ref[:, cols], k_ref[:, cols], v_ref[:, cols], enc_allowed)
        for side, dev in enumerate((y_a, y_b)):
            copy = ctx_copy(head, y, head * 2 + side, dev)
            copy.start()
            ctx_sent.append(copy)
        if head == 0:
            sib_kv.wait_recv()
            hop(1, *ring_key).start()
            hop(1, *ring_val).start()

    pass_on(1, ring_wo, fan_wo)
    ctx_copy(0, ya, 0, y_a).wait_recv()
    ctx_sent.append(ctx_copy(0, ya, 4, y_b))
    ctx_sent[-1].start()
    ctx_copy(1, yb, 3, y_b).wait_recv()
    ctx_sent.append(ctx_copy(1, yb, 5, y_a))
    ctx_sent[-1].start()

    for i in range(FEAT // 128):
        cols = slice(i * 128, (i + 1) * 128)
        hid_t[cols, :] = jnp.transpose(hid[:, cols].astype(F32))
    for h in range(1, STEPS + 1):
        p0, p1 = pair(h)
        hid_c[h - 1] = jnp.concatenate([hid_t[block(p0), :], hid_t[block(p1), :]], axis=0).astype(BF16)

    @pl.when(jnp.logical_not(off_diagonal))
    def _():
        for h in range(1, STEPS + 1):
            hid_in[h - 1, y] = hid_c[h - 1]

    @pl.when(off_diagonal)
    def _():
        hid_copy(1).start()
        hid_copy(2).start()

    pass_on(2, ring_wo, fan_wo)
    pass_on(1, ring_key, fan_key)
    pass_on(1, ring_val, fan_val)
    for i in range(FEAT // 128):
        cols = slice(i * 128, (i + 1) * 128)
        row = gain_ref[pl.ds(y * (FEAT // 128) + i, 1), :]
        column = jnp.sum(jnp.where(diag, row, 0.0), axis=1, keepdims=True)
        gain_col[cols, :] = jnp.broadcast_to(column, (128, 128))
    acc[...] = jnp.zeros_like(acc)
    sums[...] = jnp.zeros_like(sums)
    ctx_copy(0, yb, 1, y_b).wait_recv()
    ctx_copy(1, ya, 2, y_a).wait_recv()
    ctx_copy(0, y2, 4, y_b).wait_recv()
    ctx_copy(1, y2, 5, y_a).wait_recv()

    def kv_weights(i, s):
        blocks = pair(2 * s + 1) + pair(2 * s + 2)
        return jnp.concatenate([kvw[i, block(p), :] for p in blocks], axis=0)

    @pl.loop(1, STEPS + 5)
    def _(h):
        @pl.when(h <= STEPS - 2)
        def _():
            pass_on(h + 2, ring_wo, fan_wo)

            @pl.when(off_diagonal)
            def _():
                hid_copy(h + 2).start()

        @pl.when((h >= 3) & (h <= STEPS + 2))
        def _():
            t = h - 2
            for copy in round_one(t):
                copy.wait_recv()
            total = part[t - 1] + x1r[t - 1].astype(F32)
            part[t - 1] = total
            x2s[t - 1] = total.astype(BF16)
            for copy in round_two(t):
                copy.start()

        @pl.when(h < STEPS)
        def _():
            pass_on(h + 1, ring_key, fan_key)

        @pl.when(h <= STEPS)
        def _():
            @pl.when(h < STEPS)
            def _():
                fan_got(h, *fan_wo).wait_recv()

            p0, p1 = pair(h)
            weights = jnp.concatenate([wo[block(p0), :], wo[block(p1), :]], axis=0)
            part[h - 1] = nt(weights[:, 0:HEAD_DIM], ctx[0].reshape(GROUP, HEAD_DIM)) + nt(
                weights[:, HEAD_DIM:WID], ctx[1].reshape(GROUP, HEAD_DIM)
            )

            @pl.when(jnp.logical_not(off_diagonal))
            def _():
                for d in range(1, NY):
                    hid_got(h, d).wait_recv()
                for g in range(NY):
                    rows = slice(g * ROWS, (g + 1) * ROWS)
                    part[h - 1, :, rows] = part[h - 1, :, rows] + hid_in[h - 1, g].astype(F32)

            x1s[h - 1] = part[h - 1].astype(BF16)
            for copy in round_one(h):
                copy.start()

            @pl.when(h < STEPS)
            def _():
                pass_on(h + 1, ring_val, fan_val)

        @pl.when(h >= 5)
        def _():
            t = h - 4
            for copy in round_two(t):
                copy.wait_recv()
            p0, p1 = pair(t)
            total = part[t - 1] + x2r[t - 1].astype(F32)
            part[t - 1] = total
            sums[...] += jnp.sum(total * total, axis=0, keepdims=True)
            gain = jnp.concatenate([gain_col[block(p0), :], gain_col[block(p1), :]], axis=0)
            total = total * jnp.concatenate([gain] * NY, axis=1)
            at = pl.ds(pl.multiple_of(((t - 1) % 2) * 128, 128), 128)
            res_t[(t - 1) // 2, :, at] = jnp.transpose(total).astype(BF16)

            @pl.when(jnp.logical_not(off_diagonal))
            def _():
                for g in range(NY):
                    out_c[t - 1, g] = part[t - 1, :, g * ROWS : (g + 1) * ROWS].astype(BF16)
                for d in range(1, NY):
                    out_copy(t, d).start()
                out_in[t - 1] = out_c[t - 1, y]

            @pl.when(t < STEPS)
            def _():
                fan_got(t, *fan_key).wait_recv()
                fan_got(t, *fan_val).wait_recv()

            @pl.when((t % 2 == 0) & (t < STEPS))
            def _():
                s = t // 2 - 1
                for i in range(2):
                    acc[i] += nn(res_t[s], kv_weights(i, s)).reshape(NY, ROWS, WID)

    def lanes(g):
        return pl.ds(pl.multiple_of(g * ROWS, ROWS), ROWS)

    def finished(i, g):
        s = STEPS // 2 - 1
        return acc[i, g] + nn(res_t[s, lanes(g), :], kv_weights(i, s))

    y_copies = [remote(ys.at[i], yr.at[i], y_s.at[i], y_r.at[i], (y_a, y_b)[i % 2]) for i in range(6)]
    ys[0] = finished(0, y2).astype(BF16)
    y_copies[0].start()
    ys[1] = finished(1, y2).astype(BF16)
    y_copies[1].start()
    ys[2] = finished(0, ya).astype(BF16)
    y_copies[2].start()
    ys[3] = finished(1, yb).astype(BF16)
    y_copies[3].start()
    stat_copies = []
    for i, (g, dev) in enumerate(((ya, y_a), (yb, y_b), (y2, y_2))):
        ss_s[i] = sums[:, lanes(g)]
        copy = remote(ss_s.at[i], ss_r.at[i], st_s.at[i], st_r.at[i], dev)
        copy.start()
        stat_copies.append(copy)
    to_a = finished(1, ya)
    y_copies[1].wait_recv()
    ys[4] = (to_a + yr[1].astype(F32)).astype(BF16)
    y_copies[4].start()
    to_b = finished(0, yb)
    y_copies[0].wait_recv()
    ys[5] = (to_b + yr[0].astype(F32)).astype(BF16)
    y_copies[5].start()
    acc[0, y] = finished(0, y)
    acc[1, y] = finished(1, y)

    for h in range(1, STEPS + 1):
        @pl.when(off_diagonal)
        def _():
            out_copy(h, 1).wait_recv()

        p0, p1 = pair(h)
        out_t[block(p0), :] = out_in[h - 1, 0:BLK, :].astype(F32)
        out_t[block(p1), :] = out_in[h - 1, BLK : 2 * BLK, :].astype(F32)
    for i in range(FEAT // 128):
        cols = slice(i * 128, (i + 1) * 128)
        enc_out[:, cols] = jnp.transpose(out_t[cols, :]).astype(BF16)

    lower_half = rows_i < DROWS
    above_end = jnp.minimum(w + 2, NW)
    base = jnp.where(lower_half, start(ordered[1:2], dbound[w]), start(ordered[1:2], dbound[w + 1]))
    last = jnp.where(lower_half, dbound[w + 1].astype(F32), dbound[above_end].astype(F32))
    offset = (rows_i % DROWS).astype(F32)
    dec_col = tags(ends[1:2], base + offset, last)
    dec_allowed = (dec_col == enc_row) & (enc_row >= 0.0)

    for copy in stat_copies:
        copy.wait_recv()
    square = sums[:, lanes(y)] + ss_r[0] + ss_r[1] + ss_r[2]
    square_col = jnp.sum(jnp.where(diag, square[0:1], 0.0), axis=1, keepdims=True)
    norm = lax.rsqrt(square_col * (1.0 / (NY * FEAT)) + EPSILON)
    dq_copy.wait_recv()

    y_copies[2].wait_recv()
    y_copies[3].wait_recv()
    y_copies[4].wait_recv()
    near_values = acc[1, y] + yr[3].astype(F32) + yr[4].astype(F32)
    near_values = (near_values * norm).astype(BF16)
    y_copies[5].wait_recv()
    near_keys = acc[0, y] + yr[2].astype(F32) + yr[5].astype(F32)
    near_keys = (near_keys * norm).astype(BF16)

    def near(rows, head):
        cols = slice(head * HEAD_DIM, (head + 1) * HEAD_DIM)
        return attend(dq2[rows, cols], near_keys[:, cols], near_values[:, cols], dec_allowed[rows])

    for head in range(2):
        dres[:, head * HEAD_DIM : (head + 1) * HEAD_DIM] = near(slice(DROWS, ROWS), head)
    up = remote(dres, drecv, misc_s.at[3], misc_r.at[3], upper)
    up.start()
    found = [near(slice(0, DROWS), head) for head in range(2)]

    for copy in [sib_wo, sib_kv, dq_copy] + ctx_sent + stat_copies + y_copies:
        copy.wait_send()

    @pl.loop(1, STEPS + 1)
    def _(h):
        hop(h, *ring_wo).wait_send()
        hop(h, *ring_key).wait_send()
        hop(h, *ring_val).wait_send()
        for copy in round_one(h) + round_two(h):
            copy.wait_send()

        @pl.when(h < STEPS)
        def _():
            fan(h, *fan_wo).wait_send()
            fan(h, *fan_key).wait_send()
            fan(h, *fan_val).wait_send()

        @pl.when(off_diagonal)
        def _():
            hid_copy(h).wait_send()

        @pl.when(jnp.logical_not(off_diagonal))
        def _():
            for d in range(1, NY):
                out_copy(h, d).wait_send()

    up.wait()
    cross_out[...] = jnp.concatenate(found, axis=1) + drecv[...]


def body(
    hidden_in, enc_query, enc_key, enc_value, dec_query, out_proj, key_proj, value_proj,
    norm_gain, enc_len, dec_len, example_order, enc_bounds, dec_bounds,
):
    vmem = pl.BlockSpec(memory_space=pltpu.VMEM)
    anywhere = pl.BlockSpec(memory_space=pl.ANY)
    dma = pltpu.SemaphoreType.DMA
    gain = norm_gain.reshape(32, 128)
    return pl.pallas_call(
        kernel,
        out_shape=(
            jax.ShapeDtypeStruct((ROWS, FEAT), BF16),
            jax.ShapeDtypeStruct((DROWS, WID), BF16),
        ),
        in_specs=[anywhere] * 14,
        out_specs=(vmem, vmem),
        scratch_shapes=[
            pltpu.VMEM((ROWS, WID), BF16),
            pltpu.VMEM((ROWS, WID), BF16),
            pltpu.VMEM((ROWS, WID), BF16),
            pltpu.VMEM(gain.shape, F32),
            pltpu.VMEM((FEAT, 128), F32),
            pltpu.VMEM((3, 1, 256), jnp.int32),
            pltpu.SMEM(enc_bounds.shape, jnp.int32),
            pltpu.SMEM(dec_bounds.shape, jnp.int32),
            pltpu.VMEM((FEAT, WID), BF16),
            pltpu.VMEM((2, FEAT, WID), BF16),
            pltpu.VMEM((2, NY, ROWS, HEAD_DIM), BF16),
            pltpu.VMEM((ROWS, FEAT), BF16),
            pltpu.VMEM((FEAT, ROWS), F32),
            pltpu.VMEM((STEPS, 2 * BLK, ROWS), BF16),
            pltpu.VMEM((STEPS, NY, 2 * BLK, ROWS), BF16),
            pltpu.VMEM((STEPS, 2 * BLK, GROUP), F32),
            pltpu.VMEM((STEPS, 2 * BLK, GROUP), BF16),
            pltpu.VMEM((STEPS, 2 * BLK, GROUP), BF16),
            pltpu.VMEM((STEPS, 2 * BLK, GROUP), BF16),
            pltpu.VMEM((STEPS, 2 * BLK, GROUP), BF16),
            pltpu.VMEM((STEPS // 2, GROUP, 4 * BLK), BF16),
            pltpu.VMEM((2, NY, ROWS, WID), F32),
            pltpu.VMEM((8, GROUP), F32),
            pltpu.VMEM((FEAT, ROWS), F32),
            pltpu.VMEM((STEPS, NY, 2 * BLK, ROWS), BF16),
            pltpu.VMEM((STEPS, 2 * BLK, ROWS), BF16),
            pltpu.VMEM((6, ROWS, WID), BF16),
            pltpu.VMEM((6, ROWS, WID), BF16),
            pltpu.VMEM((3, 8, ROWS), F32),
            pltpu.VMEM((3, 8, ROWS), F32),
            pltpu.VMEM((2 * DROWS, WID), BF16),
            pltpu.VMEM((DROWS, WID), BF16),
            pltpu.VMEM((DROWS, WID), BF16),
            dma((14,)),
            dma((2,)), dma((2,)),
            dma((STEPS,)), dma((STEPS,)),
            dma((STEPS,)), dma((STEPS,)),
            dma((STEPS,)), dma((STEPS,)),
            dma((STEPS,)), dma((STEPS,)),
            dma((STEPS,)), dma((STEPS,)),
            dma((STEPS,)), dma((STEPS,)),
            dma((4,)), dma((4,)),
            dma((STEPS,)), dma((STEPS, NY - 1)),
            dma((STEPS, NY - 1)), dma((STEPS,)),
            dma((6,)), dma((6,)),
            dma((STEPS, 2)), dma((STEPS, 2)),
            dma((STEPS, 2)), dma((STEPS, 2)),
            dma((6,)), dma((6,)),
            dma((3,)), dma((3,)),
        ],
        compiler_params=pltpu.CompilerParams(
            collective_id=0, has_side_effects=True, vmem_limit_bytes=VMEM_LIMIT
        ),
        name="encoder_to_cross",
    )(
        hidden_in, enc_query, enc_key, enc_value, dec_query, out_proj.T, key_proj, value_proj,
        gain, enc_len.reshape(1, 256), dec_len.reshape(1, 256),
        example_order.reshape(1, 256), enc_bounds, dec_bounds,
    )


def solution(mesh):
    return jax.shard_map(
        body,
        mesh=mesh,
        in_specs=(
            P("wide", "head"), P("wide", "head"), P("wide", "head"), P("wide", "head"),
            P("wide", "head"), P("head", "wide"), P("wide", "head"), P("wide", "head"),
            P(), P(), P(), P(), P(), P(),
        ),
        out_specs=(P("wide", "head"), P("wide", "head")),
        check_vma=False,
    )
```

time: 569 us -> 76.3 us (0.13)
  waiting for transfers between devices: 518 us -> 0 us
  Pallas kernels: 0 us -> 73.2 us
  matrix products: 13.8 us -> 0 us
  between operations: 14 us -> 0.65 us
  other arithmetic: 13.1 us -> 0 us
  starting transfers between devices: 6.49 us -> 0 us
    all_gather x4 -> x0, waiting for transfers between devices: 437 us -> none  [the longest x1 144 us: body(): lax.all_gather(key_proj, 'wide', axis=0, tiled=True)]
    psum x1 -> x0, waiting for transfers between devices: 77.8 us -> none  [body(): total_sum = lax.psum(gathered, 'head')]
    pallas_call x0 -> x1, Pallas kernels: none -> 73.2 us  [body(): pl.pallas_call(kernel, out_shape=(jax.ShapeDtypeStruct((ROWS, FEAT), BF16...]
    dot_general x6 -> x0, matrix products: 13.4 us -> none  [the longest x1 4.97 us: body(): jnp.dot(context, lax.all_gather(out_proj, 'wide', axis=1, tiled=True), pr...]
    reduce_sum x7 -> x0, other arithmetic: 8.26 us -> none  [the longest x2 3.34 us: row_tags(): row_base = jnp.sum(jnp.where(places == first_pos, start_rows, 0))]
    ppermute x2 -> x0, starting transfers between devices: 6.29 us -> none  [passed_along(): lax.ppermute(value, axis, [(source, source + steps) for source in range(i...]
  transfers between devices with their start and end apart: 7 -> 0, of which waited for: 6 -> 0; matrix products, arithmetic and copies ran while one was open for 5% -> 0% of each run, Pallas kernels for 0% -> 0%
where the time goes in v1:
time: 76.3 us; the launch traced here: 76.2 us
  Pallas kernels  73.2 us (96%)
  local copies, waits for them, and re-layouts  2.33 us (3%)
    pallas_call x1, Pallas kernels, body(): pl.pallas_call(kernel, out_shape=(jax.ShapeDtypeStruct((ROWS, FEAT), BF16...  73.2 us
    unnamed x4, local copies, waits for them, and re-layouts  2.33 us

profile of v1, /device:TPU:1, one launch (start us, length us, event | category | flops | bytes accessed | tf_op | source)
XLA Modules:
  0.0 76.2 jit_solution(14532634709407383584)
XLA Ops:
  0.6 73.2 %encoder_to_cross.1 = (bf16[128,1024]{1,0:T(8,128)(2,1)}, bf16[64,512]{1,0:T(8,128)(2,1)}) custom-call(bf16[128,1024]{1,0:T(8,128)(2,1)} %hidden.1, bf16[128,512]{1,0:T(8,128)(2,1)} %q_hbm.1, bf16[128,512]{1,0:T(8,128)(2,1)} %k_hbm.1, bf16[128,512]{1,0:T(8,128)(2,1)} %v_hbm.1, bf16[64,512]{1,0:T(8,128)(2,1)} %dq_hbm.1, bf16[32,512]{1,0:T(8,128)(2,1)} %bitcast.5, ...), custom_call_target="tpu_custom_call" | custom-call | tf_op jit(solution)/shard_map/encoder_to_cross/pallas_call | solution.py:476
  73.8 0.0 copy-start
  73.8 1.7 %copy.18 = bf16[128,1024]{1,0:T(8,128)(2,1)} copy(bf16[128,1024]{1,0:T(8,128)(2,1)} %get-tuple-element.4) | data formatting | bytes 524288
  75.5 0.0 copy-done
  75.5 0.6 copy.19
Async XLA Ops:
  73.8 1.7 %copy-start = (bf16[64,512]{1,0:T(8,128)(2,1)S(1)}, bf16[64,512]{1,0:T(8,128)(2,1)}, u32[]{:S(2)}) copy-start(bf16[64,512]{1,0:T(8,128)(2,1)} %get-tuple-element.5) | copy-start | bytes 196612

commit v2 on v1

--- a/solution.py
+++ b/solution.py
@@ -52,9 +52,9 @@
     enc_out, cross_out,
     q_ref, k_ref, v_ref, gain_ref, gain_col, lens_ref, ebound, dbound,
     wo, kvw, ctx, hid, hid_t, hid_c, hid_in, part, x1s, x1r, x2s, x2r, res_t, acc, sums, out_t, out_c, out_in,
-    ys, yr, ss_s, ss_r, dq2, dres, drecv,
+    ys, yr, ss_r, dq2, dres, drecv,
     in_sem, sib_s, sib_r, wo_s, wo_r, wof_s, wof_r, key_s, key_r, keyf_s, keyf_r,
-    val_s, val_r, valf_s, valf_r, misc_s, misc_r, hid_s, hid_r, out_s, out_r, ctx_s, ctx_r, xs1, xr1, xs2, xr2, y_s, y_r, st_s, st_r,
+    val_s, val_r, valf_s, valf_r, misc_s, misc_r, hid_s, hid_r, out_s, out_r, ctx_s, ctx_r, xs1, xr1, xs2, xr2, gs, gr, y_s, y_r, st_s, st_r,
 ):
     w = lax.axis_index("wide")
     x = lax.axis_index("head")
@@ -171,22 +171,43 @@
         low = jnp.where(h == STEPS, z, z - h)
         return low, z + h
 
+    halves = (pl.ds(0, BLK), pl.ds(BLK, BLK))
+
     def round_one(h):
         return [
             remote(
-                x1s.at[h - 1, pl.ds(half * BLK, BLK)], x1r.at[h - 1, pl.ds(half * BLK, BLK)],
-                xs1.at[h - 1, half], xr1.at[h - 1, half], (x_a, x_b)[half],
+                x1s.at[h - 1, :, rows], x1r.at[h - 1, :, rows],
+                xs1.at[h - 1, i], xr1.at[h - 1, i], (x_a, x_b)[i],
             )
-            for half in range(2)
+            for i, rows in enumerate(halves)
         ]
 
     def round_two(h):
         return [
             remote(
-                x2s.at[h - 1, pl.ds(half * BLK, BLK)], x2r.at[h - 1, pl.ds(half * BLK, BLK)],
-                xs2.at[h - 1, half], xr2.at[h - 1, half], (x_b, x_a)[half],
+                x2s.at[h - 1, :, rows], x2r.at[h - 1, :, rows],
+                xs2.at[h - 1, i], xr2.at[h - 1, i], (x_b, x_a)[i],
             )
-            for half in range(2)
+            for i, rows in enumerate(halves)
+        ]
+
+    def group_one(h, g):
+        at = 0 if h == 1 else 1
+        return [
+            remote(
+                x1s.at[h - 1, g, rows], x1r.at[h - 1, g, rows],
+                gs.at[at, g, i], gr.at[at, g, i], (x_a, x_b)[i],
+            )
+            for i, rows in enumerate(halves)
+        ]
+
+    def group_two(h, g):
+        return [
+            remote(
+                x2s.at[h - 1, g, rows], x2r.at[h - 1, g, rows],
+                gs.at[2, g, i], gr.at[2, g, i], (x_b, x_a)[i],
+            )
+            for i, rows in enumerate(halves)
         ]
 
     away = (y - x + NY) % NY
@@ -226,32 +247,76 @@
             hop(1, *ring_key).start()
             hop(1, *ring_val).start()
 
+    for i in range(FEAT // 128):
+        cols = slice(i * 128, (i + 1) * 128)
+        hid_t[cols, :] = jnp.transpose(hid[:, cols].astype(F32))
+
+    def of_pair(ref, h):
+        p0, p1 = pair(h)
+        return jnp.concatenate([ref[block(p0), :], ref[block(p1), :]], axis=0)
+
+    @pl.loop(1, STEPS + 1)
+    def _(h):
+        hid_c[h - 1] = of_pair(hid_t, h).astype(BF16)
+
+    @pl.when(off_diagonal)
+    def _():
+        hid_copy(1).start()
+        hid_copy(2).start()
+
+    @pl.when(jnp.logical_not(off_diagonal))
+    def _():
+        for h in range(1, STEPS + 1):
+            hid_in[h - 1, y] = hid_c[h - 1]
+
     pass_on(1, ring_wo, fan_wo)
+
+    def project_group(h, g, d):
+        weights = of_pair(wo, h)
+        part[h - 1, g] = nt(weights[:, 0:HEAD_DIM], ctx[0, g]) + nt(weights[:, HEAD_DIM:WID], ctx[1, g])
+
+        @pl.when(jnp.logical_not(off_diagonal))
+        def _():
+            if d:
+                hid_got(h, d).wait_recv()
+            part[h - 1, g] = part[h - 1, g] + hid_in[h - 1, g].astype(F32)
+
+        x1s[h - 1, g] = part[h - 1, g].astype(BF16)
+        for copy in group_one(h, g):
+            copy.start()
+
+    d_a, d_b = (ya - y + NY) % NY, (yb - y + NY) % NY
+
+    def project_other(h, which):
+        if which == 2:
+            project_group(h, y2, 2)
+            return
+        g, d = ((ya, d_a), (yb, d_b))[which]
+        weights = of_pair(wo, h)
+        part[h - 1, g] = nt(weights[:, 0:HEAD_DIM], ctx[0, g]) + nt(weights[:, HEAD_DIM:WID], ctx[1, g])
+
+        @pl.when(jnp.logical_not(off_diagonal))
+        def _():
+            hid_got(h, d).wait_recv()
+            part[h - 1, g] = part[h - 1, g] + hid_in[h - 1, g].astype(F32)
+
+        x1s[h - 1, g] = part[h - 1, g].astype(BF16)
+        for copy in group_one(h, g):
+            copy.start()
+
+    fan_got(1, *fan_wo).wait_recv()
+    project_group(1, y, 0)
     ctx_copy(0, ya, 0, y_a).wait_recv()
     ctx_sent.append(ctx_copy(0, ya, 4, y_b))
     ctx_sent[-1].start()
     ctx_copy(1, yb, 3, y_b).wait_recv()
     ctx_sent.append(ctx_copy(1, yb, 5, y_a))
     ctx_sent[-1].start()
-
-    for i in range(FEAT // 128):
-        cols = slice(i * 128, (i + 1) * 128)
-        hid_t[cols, :] = jnp.transpose(hid[:, cols].astype(F32))
-    for h in range(1, STEPS + 1):
-        p0, p1 = pair(h)
-        hid_c[h - 1] = jnp.concatenate([hid_t[block(p0), :], hid_t[block(p1), :]], axis=0).astype(BF16)
-
-    @pl.when(jnp.logical_not(off_diagonal))
-    def _():
-        for h in range(1, STEPS + 1):
-            hid_in[h - 1, y] = hid_c[h - 1]
-
-    @pl.when(off_diagonal)
-    def _():
-        hid_copy(1).start()
-        hid_copy(2).start()
-
     pass_on(2, ring_wo, fan_wo)
+    ctx_copy(1, ya, 2, y_a).wait_recv()
+    project_other(1, 0)
+    ctx_copy(0, yb, 1, y_b).wait_recv()
+    project_other(1, 1)
     pass_on(1, ring_key, fan_key)
     pass_on(1, ring_val, fan_val)
     for i in range(FEAT // 128):
@@ -261,16 +326,70 @@
         gain_col[cols, :] = jnp.broadcast_to(column, (128, 128))
     acc[...] = jnp.zeros_like(acc)
     sums[...] = jnp.zeros_like(sums)
-    ctx_copy(0, yb, 1, y_b).wait_recv()
-    ctx_copy(1, ya, 2, y_a).wait_recv()
     ctx_copy(0, y2, 4, y_b).wait_recv()
     ctx_copy(1, y2, 5, y_a).wait_recv()
+    project_other(1, 2)
 
     def kv_weights(i, s):
         blocks = pair(2 * s + 1) + pair(2 * s + 2)
         return jnp.concatenate([kvw[i, block(p), :] for p in blocks], axis=0)
 
-    @pl.loop(1, STEPS + 5)
+    def project(h):
+        fan_got(h, *fan_wo).wait_recv()
+        weights = of_pair(wo, h)
+        term = nt(weights[:, 0:HEAD_DIM], ctx[0].reshape(GROUP, HEAD_DIM)) + nt(
+            weights[:, HEAD_DIM:WID], ctx[1].reshape(GROUP, HEAD_DIM)
+        )
+        for g in range(NY):
+            part[h - 1, g] = term[:, g * ROWS : (g + 1) * ROWS]
+
+        @pl.when(jnp.logical_not(off_diagonal))
+        def _():
+            for d in range(1, NY):
+                hid_got(h, d).wait_recv()
+            part[h - 1] = part[h - 1] + hid_in[h - 1].astype(F32)
+
+        x1s[h - 1] = part[h - 1].astype(BF16)
+        for copy in round_one(h):
+            copy.start()
+
+    def exchange(h):
+        @pl.when(h == 1)
+        def _():
+            for g in range(NY):
+                for copy in group_one(1, g):
+                    copy.wait_recv()
+
+        @pl.when(h > 1)
+        def _():
+            for copy in round_one(h):
+                copy.wait_recv()
+
+        total = part[h - 1] + x1r[h - 1].astype(F32)
+        part[h - 1] = total
+        x2s[h - 1] = total.astype(BF16)
+        for copy in round_two(h):
+            copy.start()
+
+    def finish_group(h, g):
+        total = part[h - 1, g] + x2r[h - 1, g].astype(F32)
+        sums[g] += jnp.sum(total * total, axis=0, keepdims=True)
+        at = pl.ds(pl.multiple_of(((h - 1) % 2) * 128, 128), 128)
+        res_t[(h - 1) // 2, g, :, at] = jnp.transpose(total * of_pair(gain_col, h)).astype(BF16)
+        out_c[h - 1, g] = total.astype(BF16)
+
+    def send_home(h):
+        @pl.when(jnp.logical_not(off_diagonal))
+        def _():
+            for d in range(1, NY):
+                out_copy(h, d).start()
+            out_in[h - 1] = out_c[h - 1, y]
+
+    def accumulate(s):
+        for i in range(2):
+            acc[i] += nn(res_t[s].reshape(GROUP, 4 * BLK), kv_weights(i, s)).reshape(NY, ROWS, WID)
+
+    @pl.loop(1, STEPS + 4)
     def _(h):
         @pl.when(h <= STEPS - 2)
         def _():
@@ -280,114 +399,109 @@
             def _():
                 hid_copy(h + 2).start()
 
-        @pl.when((h >= 3) & (h <= STEPS + 2))
-        def _():
-            t = h - 2
-            for copy in round_one(t):
-                copy.wait_recv()
-            total = part[t - 1] + x1r[t - 1].astype(F32)
-            part[t - 1] = total
-            x2s[t - 1] = total.astype(BF16)
-            for copy in round_two(t):
-                copy.start()
+        @pl.when((h >= 3) & (h <= STEPS + 1))
+        def _():
+            exchange(h - 2)
 
         @pl.when(h < STEPS)
         def _():
             pass_on(h + 1, ring_key, fan_key)
 
-        @pl.when(h <= STEPS)
-        def _():
-            @pl.when(h < STEPS)
+            @pl.when(h > 1)
             def _():
-                fan_got(h, *fan_wo).wait_recv()
-
-            p0, p1 = pair(h)
-            weights = jnp.concatenate([wo[block(p0), :], wo[block(p1), :]], axis=0)
-            part[h - 1] = nt(weights[:, 0:HEAD_DIM], ctx[0].reshape(GROUP, HEAD_DIM)) + nt(
-                weights[:, HEAD_DIM:WID], ctx[1].reshape(GROUP, HEAD_DIM)
-            )
-
-            @pl.when(jnp.logical_not(off_diagonal))
-            def _():
-                for d in range(1, NY):
-                    hid_got(h, d).wait_recv()
-                for g in range(NY):
-                    rows = slice(g * ROWS, (g + 1) * ROWS)
-                    part[h - 1, :, rows] = part[h - 1, :, rows] + hid_in[h - 1, g].astype(F32)
-
-            x1s[h - 1] = part[h - 1].astype(BF16)
-            for copy in round_one(h):
-                copy.start()
-
-            @pl.when(h < STEPS)
-            def _():
-                pass_on(h + 1, ring_val, fan_val)
+                project(h)
+
+            pass_on(h + 1, ring_val, fan_val)
+
+        @pl.when(h == STEPS)
+        def _():
+            for which in (2, 0, 1):
+                project_other(STEPS, which)
+            project_group(STEPS, y, 0)
+
+        @pl.when(h == STEPS + 2)
+        def _():
+            for g in (y2, ya, yb, y):
+                for copy in group_one(STEPS, g):
+                    copy.wait_recv()
+                total = part[STEPS - 1, g] + x1r[STEPS - 1, g].astype(F32)
+                part[STEPS - 1, g] = total
+                x2s[STEPS - 1, g] = total.astype(BF16)
+                for copy in group_two(STEPS, g):
+                    copy.start()
 
         @pl.when(h >= 5)
         def _():
             t = h - 4
             for copy in round_two(t):
                 copy.wait_recv()
-            p0, p1 = pair(t)
-            total = part[t - 1] + x2r[t - 1].astype(F32)
-            part[t - 1] = total
-            sums[...] += jnp.sum(total * total, axis=0, keepdims=True)
-            gain = jnp.concatenate([gain_col[block(p0), :], gain_col[block(p1), :]], axis=0)
-            total = total * jnp.concatenate([gain] * NY, axis=1)
-            at = pl.ds(pl.multiple_of(((t - 1) % 2) * 128, 128), 128)
-            res_t[(t - 1) // 2, :, at] = jnp.transpose(total).astype(BF16)
-
-            @pl.when(jnp.logical_not(off_diagonal))
+
+            @pl.loop(0, NY)
+            def _(g):
+                finish_group(t, g)
+
+            send_home(t)
+            fan_got(t, *fan_key).wait_recv()
+            fan_got(t, *fan_val).wait_recv()
+
+            @pl.when(t % 2 == 0)
             def _():
-                for g in range(NY):
-                    out_c[t - 1, g] = part[t - 1, :, g * ROWS : (g + 1) * ROWS].astype(BF16)
-                for d in range(1, NY):
-                    out_copy(t, d).start()
-                out_in[t - 1] = out_c[t - 1, y]
-
-            @pl.when(t < STEPS)
-            def _():
-                fan_got(t, *fan_key).wait_recv()
-                fan_got(t, *fan_val).wait_recv()
-
-            @pl.when((t % 2 == 0) & (t < STEPS))
-            def _():
-                s = t // 2 - 1
-                for i in range(2):
-                    acc[i] += nn(res_t[s], kv_weights(i, s)).reshape(NY, ROWS, WID)
-
-    def lanes(g):
-        return pl.ds(pl.multiple_of(g * ROWS, ROWS), ROWS)
-
-    def finished(i, g):
+                accumulate(t // 2 - 1)
+
+    def head_cols(head):
+        return slice(head * HEAD_DIM, (head + 1) * HEAD_DIM)
+
+    def finished(i, g, head):
         s = STEPS // 2 - 1
-        return acc[i, g] + nn(res_t[s, lanes(g), :], kv_weights(i, s))
-
-    y_copies = [remote(ys.at[i], yr.at[i], y_s.at[i], y_r.at[i], (y_a, y_b)[i % 2]) for i in range(6)]
-    ys[0] = finished(0, y2).astype(BF16)
-    y_copies[0].start()
-    ys[1] = finished(1, y2).astype(BF16)
-    y_copies[1].start()
-    ys[2] = finished(0, ya).astype(BF16)
-    y_copies[2].start()
-    ys[3] = finished(1, yb).astype(BF16)
-    y_copies[3].start()
+        return acc[i, g, :, head_cols(head)] + nn(res_t[s, g], kv_weights(i, s)[:, head_cols(head)])
+
+    def last_group(g):
+        for copy in group_two(STEPS, g):
+            copy.wait_recv()
+        finish_group(STEPS, g)
+
+    def y_copy(i, head):
+        return remote(
+            ys.at[i, head], yr.at[i, head], y_s.at[i, head], y_r.at[i, head], (y_a, y_b)[i % 2]
+        )
+
+    def y_send(i, head, value):
+        ys[i, head] = value.astype(BF16)
+        y_copy(i, head).start()
+
+    def y_read(i, head):
+        return yr[i, head].astype(F32)
+
+    def relay(head):
+        to_a = finished(1, ya, head)
+        y_copy(1, head).wait_recv()
+        y_send(4, head, to_a + y_read(1, head))
+        to_b = finished(0, yb, head)
+        y_copy(0, head).wait_recv()
+        y_send(5, head, to_b + y_read(0, head))
+
+    last_group(y2)
+    for head in range(2):
+        y_send(0, head, finished(0, y2, head))
+        y_send(1, head, finished(1, y2, head))
+    last_group(ya)
+    y_send(2, 0, finished(0, ya, 0))
+    last_group(yb)
+    y_send(3, 0, finished(1, yb, 0))
+    relay(0)
+    y_send(2, 1, finished(0, ya, 1))
+    y_send(3, 1, finished(1, yb, 1))
     stat_copies = []
     for i, (g, dev) in enumerate(((ya, y_a), (yb, y_b), (y2, y_2))):
-        ss_s[i] = sums[:, lanes(g)]
-        copy = remote(ss_s.at[i], ss_r.at[i], st_s.at[i], st_r.at[i], dev)
+        copy = remote(sums.at[g], ss_r.at[i], st_s.at[i], st_r.at[i], dev)
         copy.start()
         stat_copies.append(copy)
-    to_a = finished(1, ya)
-    y_copies[1].wait_recv()
-    ys[4] = (to_a + yr[1].astype(F32)).astype(BF16)
-    y_copies[4].start()
-    to_b = finished(0, yb)
-    y_copies[0].wait_recv()
-    ys[5] = (to_b + yr[0].astype(F32)).astype(BF16)
-    y_copies[5].start()
-    acc[0, y] = finished(0, y)
-    acc[1, y] = finished(1, y)
+    relay(1)
+    last_group(y)
+    send_home(STEPS)
+    for head in range(2):
+        for i in range(2):
+            acc[i, y, :, head_cols(head)] = finished(i, y, head)
 
     for h in range(1, STEPS + 1):
         @pl.when(off_diagonal)
@@ -411,43 +525,56 @@
 
     for copy in stat_copies:
         copy.wait_recv()
-    square = sums[:, lanes(y)] + ss_r[0] + ss_r[1] + ss_r[2]
+    square = sums[y] + ss_r[0] + ss_r[1] + ss_r[2]
     square_col = jnp.sum(jnp.where(diag, square[0:1], 0.0), axis=1, keepdims=True)
     norm = lax.rsqrt(square_col * (1.0 / (NY * FEAT)) + EPSILON)
     dq_copy.wait_recv()
 
-    y_copies[2].wait_recv()
-    y_copies[3].wait_recv()
-    y_copies[4].wait_recv()
-    near_values = acc[1, y] + yr[3].astype(F32) + yr[4].astype(F32)
-    near_values = (near_values * norm).astype(BF16)
-    y_copies[5].wait_recv()
-    near_keys = acc[0, y] + yr[2].astype(F32) + yr[5].astype(F32)
-    near_keys = (near_keys * norm).astype(BF16)
-
-    def near(rows, head):
-        cols = slice(head * HEAD_DIM, (head + 1) * HEAD_DIM)
-        return attend(dq2[rows, cols], near_keys[:, cols], near_values[:, cols], dec_allowed[rows])
-
+    def up_copy(head):
+        return remote(
+            dres.at[head], drecv.at[head], misc_s.at[2 + head], misc_r.at[2 + head], upper
+        )
+
+    found = []
     for head in range(2):
-        dres[:, head * HEAD_DIM : (head + 1) * HEAD_DIM] = near(slice(DROWS, ROWS), head)
-    up = remote(dres, drecv, misc_s.at[3], misc_r.at[3], upper)
-    up.start()
-    found = [near(slice(0, DROWS), head) for head in range(2)]
-
-    for copy in [sib_wo, sib_kv, dq_copy] + ctx_sent + stat_copies + y_copies:
+        cols = head_cols(head)
+        for i in (2, 3, 4, 5):
+            y_copy(i, head).wait_recv()
+        near_keys = acc[0, y, :, cols] + y_read(2, head) + y_read(5, head)
+        near_values = acc[1, y, :, cols] + y_read(3, head) + y_read(4, head)
+        both = attend(
+            dq2[:, cols], (near_keys * norm).astype(BF16), (near_values * norm).astype(BF16), dec_allowed
+        )
+        dres[head] = both[DROWS:ROWS]
+        up_copy(head).start()
+        found.append(both[0:DROWS])
+
+    for copy in [sib_wo, sib_kv, dq_copy] + ctx_sent + stat_copies:
         copy.wait_send()
+    for head in range(2):
+        for i in range(6):
+            y_copy(i, head).wait_send()
+
+    @pl.loop(0, NY)
+    def _(g):
+        for copy in group_one(1, g) + group_one(STEPS, g) + group_two(STEPS, g):
+            copy.wait_send()
 
     @pl.loop(1, STEPS + 1)
     def _(h):
         hop(h, *ring_wo).wait_send()
         hop(h, *ring_key).wait_send()
         hop(h, *ring_val).wait_send()
-        for copy in round_one(h) + round_two(h):
-            copy.wait_send()
+
+        @pl.when((h > 1) & (h < STEPS))
+        def _():
+            for copy in round_one(h):
+                copy.wait_send()
 
         @pl.when(h < STEPS)
         def _():
+            for copy in round_two(h):
+                copy.wait_send()
             fan(h, *fan_wo).wait_send()
             fan(h, *fan_key).wait_send()
             fan(h, *fan_val).wait_send()
@@ -461,8 +588,9 @@
             for d in range(1, NY):
                 out_copy(h, d).wait_send()
 
-    up.wait()
-    cross_out[...] = jnp.concatenate(found, axis=1) + drecv[...]
+    for head in range(2):
+        up_copy(head).wait()
+        cross_out[:, head_cols(head)] = found[head] + drecv[head]
 
 
 def body(
@@ -497,24 +625,23 @@
             pltpu.VMEM((FEAT, ROWS), F32),
             pltpu.VMEM((STEPS, 2 * BLK, ROWS), BF16),
             pltpu.VMEM((STEPS, NY, 2 * BLK, ROWS), BF16),
-            pltpu.VMEM((STEPS, 2 * BLK, GROUP), F32),
-            pltpu.VMEM((STEPS, 2 * BLK, GROUP), BF16),
-            pltpu.VMEM((STEPS, 2 * BLK, GROUP), BF16),
-            pltpu.VMEM((STEPS, 2 * BLK, GROUP), BF16),
-            pltpu.VMEM((STEPS, 2 * BLK, GROUP), BF16),
-            pltpu.VMEM((STEPS // 2, GROUP, 4 * BLK), BF16),
+            pltpu.VMEM((STEPS, NY, 2 * BLK, ROWS), F32),
+            pltpu.VMEM((STEPS, NY, 2 * BLK, ROWS), BF16),
+            pltpu.VMEM((STEPS, NY, 2 * BLK, ROWS), BF16),
+            pltpu.VMEM((STEPS, NY, 2 * BLK, ROWS), BF16),
+            pltpu.VMEM((STEPS, NY, 2 * BLK, ROWS), BF16),
+            pltpu.VMEM((STEPS // 2, NY, ROWS, 4 * BLK), BF16),
             pltpu.VMEM((2, NY, ROWS, WID), F32),
-            pltpu.VMEM((8, GROUP), F32),
+            pltpu.VMEM((NY, 8, ROWS), F32),
             pltpu.VMEM((FEAT, ROWS), F32),
             pltpu.VMEM((STEPS, NY, 2 * BLK, ROWS), BF16),
             pltpu.VMEM((STEPS, 2 * BLK, ROWS), BF16),
-            pltpu.VMEM((6, ROWS, WID), BF16),
-            pltpu.VMEM((6, ROWS, WID), BF16),
-            pltpu.VMEM((3, 8, ROWS), F32),
+            pltpu.VMEM((6, 2, ROWS, HEAD_DIM), BF16),
+            pltpu.VMEM((6, 2, ROWS, HEAD_DIM), BF16),
             pltpu.VMEM((3, 8, ROWS), F32),
             pltpu.VMEM((2 * DROWS, WID), BF16),
-            pltpu.VMEM((DROWS, WID), BF16),
-            pltpu.VMEM((DROWS, WID), BF16),
+            pltpu.VMEM((2, DROWS, HEAD_DIM), BF16),
+            pltpu.VMEM((2, DROWS, HEAD_DIM), BF16),
             dma((14,)),
             dma((2,)), dma((2,)),
             dma((STEPS,)), dma((STEPS,)),
@@ -529,7 +656,8 @@
             dma((6,)), dma((6,)),
             dma((STEPS, 2)), dma((STEPS, 2)),
             dma((STEPS, 2)), dma((STEPS, 2)),
-            dma((6,)), dma((6,)),
+            dma((3, NY, 2)), dma((3, NY, 2)),
+            dma((6, 2)), dma((6, 2)),
             dma((3,)), dma((3,)),
         ],
         compiler_params=pltpu.CompilerParams(

time: 76.3 us -> 75.2 us (0.986)
  Pallas kernels: 73.2 us -> 72 us
    pallas_call x1, Pallas kernels: 73.2 us -> 72 us  [body(): pl.pallas_call(kernel, out_shape=(jax.ShapeDtypeStruct((ROWS, FEAT), BF16...]
where the time goes in v2:
time: 75.2 us; the launch traced here: 75 us
  Pallas kernels  72 us (96%)
  local copies, waits for them, and re-layouts  2.33 us (3%)
    pallas_call x1, Pallas kernels, body(): pl.pallas_call(kernel, out_shape=(jax.ShapeDtypeStruct((ROWS, FEAT), BF16...  72 us
    unnamed x4, local copies, waits for them, and re-layouts  2.33 us

profile of v2, /device:TPU:1, one launch (start us, length us, event | category | flops | bytes accessed | tf_op | source)
XLA Modules:
  0.0 75.0 jit_solution(1719316260611377135)
XLA Ops:
  0.6 72.0 %encoder_to_cross.1 = (bf16[128,1024]{1,0:T(8,128)(2,1)}, bf16[64,512]{1,0:T(8,128)(2,1)}) custom-call(bf16[128,1024]{1,0:T(8,128)(2,1)} %hidden.1, bf16[128,512]{1,0:T(8,128)(2,1)} %q_hbm.1, bf16[128,512]{1,0:T(8,128)(2,1)} %k_hbm.1, bf16[128,512]{1,0:T(8,128)(2,1)} %v_hbm.1, bf16[64,512]{1,0:T(8,128)(2,1)} %dq_hbm.1, bf16[32,512]{1,0:T(8,128)(2,1)} %bitcast.5, ...), custom_call_target="tpu_custom_call" | custom-call | tf_op jit(solution)/shard_map/encoder_to_cross/pallas_call | solution.py:604
  72.7 0.0 copy-start
  72.7 1.7 %copy.18 = bf16[128,1024]{1,0:T(8,128)(2,1)} copy(bf16[128,1024]{1,0:T(8,128)(2,1)} %get-tuple-element.4) | data formatting | bytes 524288
  74.4 0.0 copy-done
  74.4 0.6 copy.19
Async XLA Ops:
  72.7 1.7 %copy-start = (bf16[64,512]{1,0:T(8,128)(2,1)S(1)}, bf16[64,512]{1,0:T(8,128)(2,1)}, u32[]{:S(2)}) copy-start(bf16[64,512]{1,0:T(8,128)(2,1)} %get-tuple-element.5) | copy-start | bytes 196612

commit v3 on v0

v3 whole, which is shorter than its diff:
```python
import jax
import jax.numpy as jnp
from jax import lax
from jax.experimental import pallas as pl
from jax.experimental.pallas import tpu as pltpu
from jax.sharding import PartitionSpec as P

MESH = pl.DeviceIdType.MESH
F32 = jnp.float32
BF16 = jnp.bfloat16

HEAD_DIM = 256
NZ = 16
NY = 4
NX = 4
NW = NY * NZ * 2
ROWS = 128
DROWS = 64
WID = 512
PIECE = 32
BLK = 2 * PIECE
FEAT = NZ * BLK
LANES = FEAT // 128
HOPS = NZ // 2
STEPS = NZ // 4
UNITS = STEPS * NY
GROUP = NY * ROWS
EPSILON = 1e-06
SCALE = 1.0 / 16.0
VMEM_LIMIT = 60 * 1024 * 1024


def nt(a, b):
    return lax.dot_general(a, b, (((1,), (1,)), ((), ())), preferred_element_type=F32)


def nn(a, b):
    return lax.dot_general(a, b, (((1,), (0,)), ((), ())), preferred_element_type=F32)


def iota(shape, dim):
    return lax.broadcasted_iota(jnp.int32, shape, dim)


def attend(q, k, v, allowed):
    scores = jnp.where(allowed, nt(q, k) * SCALE, -1e30)
    weights = jnp.where(allowed, jnp.exp(scores - jnp.max(scores, axis=1, keepdims=True)), 0.0)
    total = jnp.maximum(jnp.sum(weights, axis=1, keepdims=True), 1.0)
    return nn((weights / total).astype(BF16), v).astype(BF16)


def kernel(
    hidden, q_hbm, k_hbm, v_hbm, dq_hbm, wo_hbm, wk_hbm, wv_hbm, gain_hbm,
    elen_hbm, dlen_hbm, order_hbm, ebound_hbm, dbound_hbm,
    enc_out, cross_out,
    q_ref, k_ref, v_ref, gain_ref, gain_c, lens_ref, ebound, dbound,
    wo, kvw, ctx, hid, hid_c, hid_in, part, x1s, x1r, x2s, x2r, res, acc, sums, out_c, out_in, out_w,
    ys, yr, st, str_, dq2, dres, drecv,
    in_sem, first_s, first_r, wo_s, wo_r, wof_s, wof_r, kv_s, kv_r, kvf_s, kvf_r,
    dq_s, dq_r, up_s, up_r, hid_s, hid_r, out_s, out_r, ctx_s, ctx_r, xs1, xr1, xs2, xr2,
    y_s, y_r, st_s, st_r,
):
    w = lax.axis_index("wide")
    x = lax.axis_index("head")
    c = w % 2
    z = (w // 2) % NZ
    y = w // (2 * NZ)
    step_dir = 1 - 2 * c

    def wide(yy, zz, cc):
        return (yy * NZ + zz) * 2 + cc

    sib = (w + step_dir, x)
    z_next = (wide(y, (z + step_dir + NZ) % NZ, c), x)
    z_prev = (wide(y, (z - step_dir + NZ) % NZ, c), x)
    ya, yb, y2 = y + 1 - 2 * (y % 2), NY - 1 - y, (y + 2) % NY
    y_a, y_b, y_2 = (wide(ya, z, c), x), (wide(yb, z, c), x), (wide(y2, z, c), x)
    x_a, x_b = (w, x + 1 - 2 * (x % 2)), (w, NX - 1 - x)
    upper, lower = ((w + 1) % NW, x), ((w + NW - 1) % NW, x)
    adder = (wide(x, z, c), x)
    off_diagonal = x != y
    near = (y_2, y_a, y_b)
    relation = jnp.where(ya == x, 1, jnp.where(yb == x, 2, 0))
    own = NY - 1
    cross = (wide(y, (z - step_dir + NZ) % NZ, 1 - c), x)
    greet = (sib, z_next, z_prev, cross, y_a, y_b, y_2, x_a, x_b, upper, lower)

    def remote(src, dst, ss, rs, dev):
        return pltpu.make_async_remote_copy(
            src_ref=src, dst_ref=dst, send_sem=ss, recv_sem=rs, device_id=dev, device_id_type=MESH
        )

    def cols_of(i, width):
        return pl.ds(pl.multiple_of(i * width, width), width)

    barrier = pltpu.get_barrier_semaphore()
    for dev in greet:
        pl.semaphore_signal(barrier, inc=1, device_id=dev, device_id_type=MESH)

    piece = cols_of(c, PIECE)
    mine = pl.ds(pl.multiple_of(z * BLK + c * PIECE, PIECE), PIECE)
    pairs = (
        (wk_hbm, kvw.at[z, 0, piece]), (wv_hbm, kvw.at[z, 1, piece]),
        (hidden, hid.at[:, pl.ds(0, FEAT)]), (hidden, hid.at[:, pl.ds(FEAT, FEAT)]), (wo_hbm, wo.at[mine]),
        (elen_hbm, lens_ref.at[0]), (dlen_hbm, lens_ref.at[1]), (order_hbm, lens_ref.at[2]),
        (ebound_hbm, ebound), (dbound_hbm, dbound),
        (q_hbm, q_ref), (k_hbm, k_ref), (v_hbm, v_ref),
        (gain_hbm, gain_ref), (dq_hbm, dq2.at[pl.ds(0, DROWS)]),
    )
    loads = [pltpu.make_async_copy(a, b, in_sem.at[i]) for i, (a, b) in enumerate(pairs)]
    for load in loads:
        load.start()

    pl.semaphore_wait(barrier, len(greet))

    around = (z_next, cross, sib)
    wo_first = [
        remote(wo_hbm, wo.at[mine], first_s.at[i], first_r.at[i], dev) for i, dev in enumerate(around)
    ]
    kv_first = [
        remote(kvw.at[z, :, piece], kvw.at[z, :, piece], first_s.at[3 + i], first_r.at[3 + i], dev)
        for i, dev in enumerate(around)
    ]
    for copy in wo_first:
        copy.start()
    for load in loads[:2]:
        load.wait()
    for copy in kv_first:
        copy.start()
    dq_copy = remote(dq_hbm, dq2.at[pl.ds(DROWS, DROWS)], dq_s, dq_r, lower)
    dq_copy.start()

    def turned(ref, by):
        wider = ref[:, pl.ds(pl.multiple_of((by // 2) * 128, 128), FEAT + 128)].astype(F32)
        return jnp.where(by % 2 == 1, wider[:, BLK : BLK + FEAT], wider[:, 0:FEAT])

    def sides(s):
        return slice(s * 128, (s + 1) * 128), slice((LANES - 1 - s) * 128, (LANES - s) * 128)

    def hid_copy(s):
        return remote(hid_c.at[s], hid_in.at[s, relation], hid_s.at[s], hid_r.at[s, relation], adder)

    def hid_got(s, r):
        return remote(hid_in.at[s, r], hid_in.at[s, r], hid_s.at[s], hid_r.at[s, r], adder)

    def out_copy(s, r):
        return remote(out_c.at[s, r], out_in.at[s], out_s.at[s, r], out_r.at[s], near[r])

    for load in loads[2:4]:
        load.wait()
    hid_turned = turned(hid, z)
    for s in range(STEPS):
        for half, cols in enumerate(sides(s)):
            hid_c[s, half] = hid_turned[:, cols].astype(BF16)

    @pl.when(off_diagonal)
    def _():
        hid_copy(0).start()
        hid_in[:, own] = jnp.zeros_like(hid_c)

    @pl.when(jnp.logical_not(off_diagonal))
    def _():
        hid_in[:, own] = hid_c[...]

    for load in loads[4:10]:
        load.wait()

    n = 256
    onehot = jnp.where(lens_ref[2] == iota((n, n), 0), 1.0, 0.0).astype(BF16)
    lens = jnp.concatenate([lens_ref[0], lens_ref[1], jnp.zeros((6, n), jnp.int32)], axis=0)
    ordered = nn(lens.astype(F32).astype(BF16), onehot)
    upto = jnp.where(iota((n, n), 0) <= iota((n, n), 1), 1.0, 0.0).astype(BF16)
    ends = nn(ordered.astype(BF16), upto)
    place = iota((1, n), 1)

    def start(row, first):
        return jnp.sum(jnp.where(place < first, row, 0.0), axis=1, keepdims=True)

    def tags(ends_row, offsets, last):
        pos = jnp.sum(jnp.where(ends_row <= offsets, 1.0, 0.0), axis=1, keepdims=True)
        return jnp.where(pos < last, pos, -1.0)

    rows_i = iota((ROWS, 1), 0)
    enc_base = start(ordered[0:1], ebound[w])
    enc_col = tags(ends[0:1], enc_base + rows_i.astype(F32), ebound[w + 1].astype(F32))
    diag = iota((ROWS, ROWS), 0) == iota((ROWS, ROWS), 1)
    enc_row = jnp.sum(jnp.where(diag, enc_col, 0.0), axis=0, keepdims=True)
    enc_allowed = (enc_col == enc_row) & (enc_row >= 0.0)

    def number(i):
        return (i + 2 * NZ) % NZ

    def wo_block(i):
        return wo.at[cols_of(number(i), BLK)]

    def kv_block(i):
        return kvw.at[number(i)]

    def hop(i, buffer, ss, rs):
        at = buffer(z - step_dir * (i - 1))
        return remote(at, at, ss.at[i - 1], rs.at[i - 1], z_next)

    def got(i, buffer, ss, rs):
        at = buffer(z - step_dir * i)
        return remote(at, at, ss.at[i - 1], rs.at[i - 1], z_next)

    def fan(i, buffer, ss, rs):
        at = buffer(z - step_dir * i)
        return remote(at, at, ss.at[i - 1], rs.at[i - 1], sib)

    def fan_got(i, buffer, ss, rs):
        at = buffer(z + step_dir * i)
        return remote(at, at, ss.at[i - 1], rs.at[i - 1], sib)

    ring_wo, fan_wo = (wo_block, wo_s, wo_r), (wo_block, wof_s, wof_r)
    ring_kv, fan_kv = (kv_block, kv_s, kv_r), (kv_block, kvf_s, kvf_r)

    def forward(i, ring, side):
        hop(i + 1, *ring).start()
        fan(i, *side).start()

    def pass_on(i, ring, side):
        got(i, *ring).wait_recv()

        @pl.when(i < HOPS)
        def _():
            forward(i, ring, side)

    def quad(s):
        return z + 2 * s, z + 2 * s + 1, z - 2 * s - 2, z - 2 * s - 1

    def ctx_copy(head, src, dst, index, dev):
        return remote(ctx.at[head, src], ctx.at[head, dst], ctx_s.at[index], ctx_r.at[index], dev)

    for copy in wo_first[:2]:
        copy.wait_recv()
    forward(1, ring_wo, fan_wo)
    for load in loads[10:]:
        load.wait()
    for head in range(2):
        cols = slice(head * HEAD_DIM, (head + 1) * HEAD_DIM)
        ctx[head, own] = attend(q_ref[:, cols], k_ref[:, cols], v_ref[:, cols], enc_allowed)
    ctx_sent = [
        ctx_copy(0, own, 1, 0, y_a), ctx_copy(1, own, 2, 3, y_b),
        ctx_copy(1, own, 1, 2, y_a), ctx_copy(0, own, 2, 1, y_b),
    ]
    for copy in ctx_sent:
        copy.start()
    for copy in kv_first[:2]:
        copy.wait_recv()
    forward(1, ring_kv, fan_kv)
    pass_on(2, ring_wo, fan_wo)

    ctx_copy(0, 1, 1, 0, y_a).wait_recv()
    ctx_sent.append(ctx_copy(0, 1, 0, 4, y_b))
    ctx_sent[-1].start()
    ctx_copy(1, 2, 2, 3, y_b).wait_recv()
    ctx_sent.append(ctx_copy(1, 2, 0, 5, y_a))
    ctx_sent[-1].start()

    @pl.when(off_diagonal)
    def _():
        hid_copy(1).start()
        hid_in[:, 0:own] = jnp.zeros((STEPS, own, 2, ROWS, 128), BF16)

    for i in range(2 * LANES):
        row = gain_ref[pl.ds(y * LANES + i % LANES, 1), :]
        out_w[0:8, i * 128 : (i + 1) * 128] = jnp.broadcast_to(row, (8, 128))
    gain_turned = turned(out_w.at[pl.ds(0, 8)], z)
    for s in range(STEPS):
        for half, cols in enumerate(sides(s)):
            gain_c[s, half] = gain_turned[:, cols]
    sums[...] = jnp.zeros_like(sums)

    def round_one(s, first, count, index):
        return [
            remote(
                x1s.at[s, i, pl.ds(first, count)], x1r.at[s, i, pl.ds(first, count)],
                xs1.at[index, i], xr1.at[index, i], (x_a, x_b)[i],
            )
            for i in range(2)
        ]

    def round_two(s, first, count, index):
        return [
            remote(
                x2s.at[s, i, pl.ds(first, count)], x2r.at[s, i, pl.ds(first, count)],
                xs2.at[index, i], xr2.at[index, i], (x_b, x_a)[i],
            )
            for i in range(2)
        ]

    x_sent = []

    def project(s, first, count, index):
        @pl.when(jnp.logical_not(off_diagonal))
        def _():
            for r in range(first, min(first + count, own)):
                hid_got(s, r).wait_recv()

        groups = slice(first, first + count)
        weights = jnp.concatenate([wo_block(i)[...] for i in quad(s)], axis=0)
        rows = [ctx[head, groups].reshape(count * ROWS, HEAD_DIM) for head in range(2)]
        term = nt(rows[0], weights[:, 0:HEAD_DIM]) + nt(rows[1], weights[:, HEAD_DIM:WID])
        for half in range(2):
            value = term[:, half * 128 : (half + 1) * 128].reshape(count, ROWS, 128)
            value = value + hid_in[s, groups, half].astype(F32)
            part[s, half, groups] = value
            x1s[s, half, groups] = value.astype(BF16)
        for copy in round_one(s, first, count, index):
            copy.start()
            x_sent.append(copy)

    def exchange(s, first, count, index):
        groups = slice(first, first + count)
        for half, copy in enumerate(round_one(s, first, count, index)):
            copy.wait_recv()
            total = part[s, half, groups] + x1r[s, half, groups].astype(F32)
            part[s, half, groups] = total
            x2s[s, half, groups] = total.astype(BF16)
            copy = round_two(s, first, count, index)[half]
            copy.start()
            x_sent.append(copy)

    def finish(s, first, count, index):
        groups = slice(first, first + count)
        for half, copy in enumerate(round_two(s, first, count, index)):
            copy.wait_recv()
            total = part[s, half, groups] + x2r[s, half, groups].astype(F32)
            sums[groups] += total * total
            res[s, groups, :, half * 128 : (half + 1) * 128] = (total * gain_c[s, half, 0:1, :]).astype(BF16)
            out_c[s, groups, half] = total.astype(BF16)

        @pl.when(jnp.logical_not(off_diagonal))
        def _():
            for r in range(first, min(first + count, own)):
                out_copy(s, r).start()
            if first + count > own:
                out_in[s] = out_c[s, own]

    def kv_weights(s, kind):
        return jnp.concatenate([kvw[number(i), kind] for i in quad(s)], axis=0)

    def accumulate(s, first, count):
        groups = slice(first, first + count)
        rows = res[s, groups].reshape(count * ROWS, 4 * BLK)
        for kind in range(2):
            term = nn(rows, kv_weights(s, kind)).reshape(count, ROWS, WID)
            acc[kind, groups] = term if s == 0 else acc[kind, groups] + term

    def fans(s, side):
        for i in (2 * s + 1, 2 * s + 2):
            if i < HOPS:
                fan_got(i, *side).wait_recv()

    def send_hidden(s):
        @pl.when(off_diagonal)
        def _():
            hid_copy(s).start()

    all_rows, early, late, end = (0, NY), (0, 2), (2, 2), STEPS - 1
    for copy in wo_first[2:]:
        copy.wait_recv()
    pass_on(3, ring_wo, fan_wo)
    fans(0, fan_wo)
    ctx_copy(0, 2, 2, 1, y_b).wait_recv()
    project(0, *late, 0)
    pass_on(2, ring_kv, fan_kv)
    pass_on(4, ring_wo, fan_wo)
    ctx_copy(1, 1, 1, 2, y_a).wait_recv()
    ctx_copy(0, 0, 0, 4, y_b).wait_recv()
    ctx_copy(1, 0, 0, 5, y_a).wait_recv()
    project(0, *early, 1)
    send_hidden(2)
    fans(1, fan_wo)
    project(1, *all_rows, 2)
    pass_on(5, ring_wo, fan_wo)
    pass_on(3, ring_kv, fan_kv)
    exchange(0, *late, 0)
    exchange(0, *early, 1)
    send_hidden(3)
    pass_on(6, ring_wo, fan_wo)
    pass_on(4, ring_kv, fan_kv)
    fans(2, fan_wo)
    project(2, *all_rows, 3)
    pass_on(7, ring_wo, fan_wo)
    exchange(1, *all_rows, 2)
    pass_on(5, ring_kv, fan_kv)
    finish(0, *late, 0)
    finish(0, *early, 1)
    pass_on(8, ring_wo, fan_wo)
    fans(3, fan_wo)
    project(3, *early, 4)
    project(3, *late, 5)
    pass_on(6, ring_kv, fan_kv)
    for copy in kv_first[2:]:
        copy.wait_recv()
    fans(0, fan_kv)
    accumulate(0, *all_rows)
    exchange(2, *all_rows, 3)
    pass_on(7, ring_kv, fan_kv)
    finish(1, *all_rows, 2)
    fans(1, fan_kv)
    accumulate(1, *all_rows)
    exchange(3, *early, 4)
    exchange(3, *late, 5)
    pass_on(8, ring_kv, fan_kv)
    finish(2, *all_rows, 3)
    fans(2, fan_kv)
    accumulate(2, *all_rows)
    fans(3, fan_kv)

    y_copies = [remote(ys.at[i], yr.at[i], y_s.at[i], y_r.at[i], (y_a, y_b)[i % 2]) for i in range(6)]

    def y_send(i, value):
        ys[i] = value.astype(BF16)
        y_copies[i].start()

    def y_read(i):
        return yr[i].astype(F32)

    finish(end, *early, 4)
    accumulate(end, *early)
    y_send(0, acc[0, 0])
    y_send(1, acc[1, 0])
    y_send(2, acc[0, 1])
    finish(end, *late, 5)
    accumulate(end, *late)
    y_send(3, acc[1, 2])
    y_copies[1].wait_recv()
    y_send(4, acc[1, 1] + y_read(1))
    y_copies[0].wait_recv()
    y_send(5, acc[0, 2] + y_read(0))

    columns = jnp.sum(sums[...], axis=2, keepdims=True)
    squares = jnp.sum(jnp.where(diag[None], columns, 0.0), axis=1, keepdims=True)
    st[...] = jnp.broadcast_to(squares, (NY, 8, ROWS))
    stat_copies = [remote(st.at[r], str_.at[r], st_s.at[r], st_r.at[r], near[r]) for r in range(own)]
    for copy in stat_copies:
        copy.start()

    @pl.when(off_diagonal)
    def _():
        for s in range(STEPS):
            out_copy(s, 0).wait_recv()

    for s in range(STEPS):
        for half, cols in enumerate(sides(s)):
            for copy in range(2):
                at = slice(cols.start + copy * FEAT, cols.stop + copy * FEAT)
                out_w[:, at] = out_in[s, half].astype(F32)
    enc_out[...] = turned(out_w, (NZ - z) % NZ).astype(BF16)

    lower_half = rows_i < DROWS
    above_end = jnp.minimum(w + 2, NW)
    base = jnp.where(lower_half, start(ordered[1:2], dbound[w]), start(ordered[1:2], dbound[w + 1]))
    last = jnp.where(lower_half, dbound[w + 1].astype(F32), dbound[above_end].astype(F32))
    offset = (rows_i % DROWS).astype(F32)
    dec_col = tags(ends[1:2], base + offset, last)
    dec_allowed = (dec_col == enc_row) & (enc_row >= 0.0)

    for copy in stat_copies:
        copy.wait_recv()
    square = st[own] + str_[0] + str_[1] + str_[2]
    square_col = jnp.sum(jnp.where(diag, square[0:1], 0.0), axis=1, keepdims=True)
    norm = lax.rsqrt(square_col * (1.0 / (NY * FEAT)) + EPSILON)
    dq_copy.wait_recv()

    for i in (2, 3, 4, 5):
        y_copies[i].wait_recv()
    near_keys = ((acc[0, own] + y_read(2) + y_read(5)) * norm).astype(BF16)
    near_values = ((acc[1, own] + y_read(3) + y_read(4)) * norm).astype(BF16)

    def cross(rows, head):
        cols = slice(head * HEAD_DIM, (head + 1) * HEAD_DIM)
        return attend(dq2[rows, cols], near_keys[:, cols], near_values[:, cols], dec_allowed[rows])

    dres[...] = jnp.concatenate([cross(slice(DROWS, ROWS), head) for head in range(2)], axis=1)
    up = remote(dres, drecv, up_s, up_r, upper)
    up.start()
    cross_out[...] = jnp.concatenate([cross(slice(0, DROWS), head) for head in range(2)], axis=1)

    for copy in wo_first + kv_first + [dq_copy] + ctx_sent + x_sent + y_copies + stat_copies:
        copy.wait_send()

    @pl.loop(1, HOPS)
    def _(i):
        hop(i + 1, *ring_wo).wait_send()
        hop(i + 1, *ring_kv).wait_send()
        fan(i, *fan_wo).wait_send()
        fan(i, *fan_kv).wait_send()

    @pl.when(off_diagonal)
    def _():
        for s in range(STEPS):
            hid_copy(s).wait_send()

    @pl.when(jnp.logical_not(off_diagonal))
    def _():
        for s in range(STEPS):
            for r in range(own):
                out_copy(s, r).wait_send()

    up.wait()
    cross_out[...] = cross_out[...] + drecv[...]


def body(
    hidden_in, enc_query, enc_key, enc_value, dec_query, out_proj, key_proj, value_proj,
    norm_gain, enc_len, dec_len, example_order, enc_bounds, dec_bounds,
):
    vmem = pl.BlockSpec(memory_space=pltpu.VMEM)
    anywhere = pl.BlockSpec(memory_space=pl.ANY)
    dma = pltpu.SemaphoreType.DMA
    gain = norm_gain.reshape(32, 128)
    square = (ROWS, 128)
    return pl.pallas_call(
        kernel,
        out_shape=(
            jax.ShapeDtypeStruct((ROWS, FEAT), BF16),
            jax.ShapeDtypeStruct((DROWS, WID), BF16),
        ),
        in_specs=[anywhere] * 14,
        out_specs=(vmem, vmem),
        scratch_shapes=[
            pltpu.VMEM((ROWS, WID), BF16),
            pltpu.VMEM((ROWS, WID), BF16),
            pltpu.VMEM((ROWS, WID), BF16),
            pltpu.VMEM(gain.shape, F32),
            pltpu.VMEM((STEPS, 2, 8, 128), F32),
            pltpu.VMEM((3, 1, 256), jnp.int32),
            pltpu.SMEM(enc_bounds.shape, jnp.int32),
            pltpu.SMEM(dec_bounds.shape, jnp.int32),
            pltpu.VMEM((FEAT, WID), BF16),
            pltpu.VMEM((NZ, 2, BLK, WID), BF16),
            pltpu.VMEM((2, NY, ROWS, HEAD_DIM), BF16),
            pltpu.VMEM((ROWS, 2 * FEAT), BF16),
            pltpu.VMEM((STEPS, 2) + square, BF16),
            pltpu.VMEM((STEPS, NY, 2) + square, BF16),
            pltpu.VMEM((STEPS, 2, NY) + square, F32),
            pltpu.VMEM((STEPS, 2, NY) + square, BF16),
            pltpu.VMEM((STEPS, 2, NY) + square, BF16),
            pltpu.VMEM((STEPS, 2, NY) + square, BF16),
            pltpu.VMEM((STEPS, 2, NY) + square, BF16),
            pltpu.VMEM((STEPS, NY, ROWS, 4 * BLK), BF16),
            pltpu.VMEM((2, NY, ROWS, WID), F32),
            pltpu.VMEM((NY,) + square, F32),
            pltpu.VMEM((STEPS, NY, 2) + square, BF16),
            pltpu.VMEM((STEPS, 2) + square, BF16),
            pltpu.VMEM((ROWS, 2 * FEAT), F32),
            pltpu.VMEM((6, ROWS, WID), BF16),
            pltpu.VMEM((6, ROWS, WID), BF16),
            pltpu.VMEM((NY, 8, ROWS), F32),
            pltpu.VMEM((NY - 1, 8, ROWS), F32),
            pltpu.VMEM((2 * DROWS, WID), BF16),
            pltpu.VMEM((DROWS, WID), BF16),
            pltpu.VMEM((DROWS, WID), BF16),
            dma((15,)),
            dma((6,)), dma((6,)),
            dma((HOPS,)), dma((HOPS,)),
            dma((HOPS,)), dma((HOPS,)),
            dma((HOPS,)), dma((HOPS,)),
            dma((HOPS,)), dma((HOPS,)),
            dma, dma,
            dma, dma,
            dma((STEPS,)), dma((STEPS, NY - 1)),
            dma((STEPS, NY - 1)), dma((STEPS,)),
            dma((6,)), dma((6,)),
            dma((STEPS + 2, 2)), dma((STEPS + 2, 2)),
            dma((STEPS + 2, 2)), dma((STEPS + 2, 2)),
            dma((6,)), dma((6,)),
            dma((NY - 1,)), dma((NY - 1,)),
        ],
        compiler_params=pltpu.CompilerParams(
            collective_id=0, has_side_effects=True, vmem_limit_bytes=VMEM_LIMIT
        ),
        name="encoder_to_cross",
    )(
        hidden_in, enc_query, enc_key, enc_value, dec_query, out_proj.T, key_proj, value_proj,
        gain, enc_len.reshape(1, 256), dec_len.reshape(1, 256),
        example_order.reshape(1, 256), enc_bounds, dec_bounds,
    )


def solution(mesh):
    return jax.shard_map(
        body,
        mesh=mesh,
        in_specs=(
            P("wide", "head"), P("wide", "head"), P("wide", "head"), P("wide", "head"),
            P("wide", "head"), P("head", "wide"), P("wide", "head"), P("wide", "head"),
            P(), P(), P(), P(), P(), P(),
        ),
        out_specs=(P("wide", "head"), P("wide", "head")),
        check_vma=False,
    )
```

time: 569 us -> 73.8 us (0.13)
  waiting for transfers between devices: 518 us -> 0 us
  Pallas kernels: 0 us -> 69.8 us
  matrix products: 13.8 us -> 0 us
  between operations: 14 us -> 0.65 us
  other arithmetic: 13.1 us -> 0 us
  starting transfers between devices: 6.49 us -> 0 us
    all_gather x4 -> x0, waiting for transfers between devices: 437 us -> none  [the longest x1 144 us: body(): lax.all_gather(key_proj, 'wide', axis=0, tiled=True)]
    psum x1 -> x0, waiting for transfers between devices: 77.8 us -> none  [body(): total_sum = lax.psum(gathered, 'head')]
    pallas_call x0 -> x1, Pallas kernels: none -> 69.8 us  [body(): pl.pallas_call(kernel, out_shape=(jax.ShapeDtypeStruct((ROWS, FEAT), BF16...]
    dot_general x6 -> x0, matrix products: 13.4 us -> none  [the longest x1 4.97 us: body(): jnp.dot(context, lax.all_gather(out_proj, 'wide', axis=1, tiled=True), pr...]
    reduce_sum x7 -> x0, other arithmetic: 8.26 us -> none  [the longest x2 3.34 us: row_tags(): row_base = jnp.sum(jnp.where(places == first_pos, start_rows, 0))]
    ppermute x2 -> x0, starting transfers between devices: 6.29 us -> none  [passed_along(): lax.ppermute(value, axis, [(source, source + steps) for source in range(i...]
  transfers between devices with their start and end apart: 7 -> 0, of which waited for: 6 -> 0; matrix products, arithmetic and copies ran while one was open for 5% -> 0% of each run, Pallas kernels for 0% -> 0%
where the time goes in v3:
time: 73.8 us; the launch traced here: 72.8 us
  Pallas kernels  69.8 us (95%)
  local copies, waits for them, and re-layouts  2.33 us (3%)
    pallas_call x1, Pallas kernels, body(): pl.pallas_call(kernel, out_shape=(jax.ShapeDtypeStruct((ROWS, FEAT), BF16...  69.8 us
    unnamed x4, local copies, waits for them, and re-layouts  2.33 us

profile of v3, /device:TPU:1, one launch (start us, length us, event | category | flops | bytes accessed | tf_op | source)
XLA Modules:
  0.0 72.8 jit_solution(9121453744523262155)
XLA Ops:
  0.6 69.8 %encoder_to_cross.1 = (bf16[128,1024]{1,0:T(8,128)(2,1)}, bf16[64,512]{1,0:T(8,128)(2,1)}) custom-call(bf16[128,1024]{1,0:T(8,128)(2,1)} %hidden.1, bf16[128,512]{1,0:T(8,128)(2,1)} %q_hbm.1, bf16[128,512]{1,0:T(8,128)(2,1)} %k_hbm.1, bf16[128,512]{1,0:T(8,128)(2,1)} %v_hbm.1, bf16[64,512]{1,0:T(8,128)(2,1)} %dq_hbm.1, bf16[32,512]{1,0:T(8,128)(2,1)} %bitcast.5, ...), custom_call_target="tpu_custom_call" | custom-call | tf_op jit(solution)/shard_map/encoder_to_cross/pallas_call | solution.py:517
  70.4 0.0 copy-start
  70.5 1.7 %copy.18 = bf16[128,1024]{1,0:T(8,128)(2,1)} copy(bf16[128,1024]{1,0:T(8,128)(2,1)} %get-tuple-element.4) | data formatting | bytes 524288
  72.2 0.0 copy-done
  72.2 0.6 copy.19
Async XLA Ops:
  70.4 1.7 %copy-start = (bf16[64,512]{1,0:T(8,128)(2,1)S(1)}, bf16[64,512]{1,0:T(8,128)(2,1)}, u32[]{:S(2)}) copy-start(bf16[64,512]{1,0:T(8,128)(2,1)} %get-tuple-element.5) | copy-start | bytes 196612

commit v4 on v3

--- a/solution.py
+++ b/solution.py
@@ -229,6 +229,50 @@
     def quad(s):
         return z + 2 * s, z + 2 * s + 1, z - 2 * s - 2, z - 2 * s - 1
 
+    def round_one(s, first, count, index):
+        return [
+            remote(
+                x1s.at[s, i, pl.ds(first, count)], x1r.at[s, i, pl.ds(first, count)],
+                xs1.at[index, i], xr1.at[index, i], (x_a, x_b)[i],
+            )
+            for i in range(2)
+        ]
+
+    def round_two(s, first, count, index):
+        return [
+            remote(
+                x2s.at[s, i, pl.ds(first, count)], x2r.at[s, i, pl.ds(first, count)],
+                xs2.at[index, i], xr2.at[index, i], (x_b, x_a)[i],
+            )
+            for i in range(2)
+        ]
+
+    x_sent = []
+
+    def project(s, first, count, index):
+        @pl.when(jnp.logical_not(off_diagonal))
+        def _():
+            for r in range(first, min(first + count, own)):
+                hid_got(s, r).wait_recv()
+
+        groups = slice(first, first + count)
+        weights = jnp.concatenate([wo_block(i)[...] for i in quad(s)], axis=0)
+        rows = [ctx[head, groups].reshape(count * ROWS, HEAD_DIM) for head in range(2)]
+        term = nt(rows[0], weights[:, 0:HEAD_DIM]) + nt(rows[1], weights[:, HEAD_DIM:WID])
+        for half in range(2):
+            value = term[:, half * 128 : (half + 1) * 128].reshape(count, ROWS, 128)
+            value = value + hid_in[s, groups, half].astype(F32)
+            part[s, half, groups] = value
+            x1s[s, half, groups] = value.astype(BF16)
+        for copy in round_one(s, first, count, index):
+            copy.start()
+            x_sent.append(copy)
+
+    def fans(s, side):
+        for i in (2 * s + 1, 2 * s + 2):
+            if i < HOPS:
+                fan_got(i, *side).wait_recv()
+
     def ctx_copy(head, src, dst, index, dev):
         return remote(ctx.at[head, src], ctx.at[head, dst], ctx_s.at[index], ctx_r.at[index], dev)
 
@@ -251,6 +295,11 @@
     forward(1, ring_kv, fan_kv)
     pass_on(2, ring_wo, fan_wo)
 
+    for copy in wo_first[2:]:
+        copy.wait_recv()
+    fans(0, fan_wo)
+    project(0, 3, 1, 0)
+
     ctx_copy(0, 1, 1, 0, y_a).wait_recv()
     ctx_sent.append(ctx_copy(0, 1, 0, 4, y_b))
     ctx_sent[-1].start()
@@ -271,45 +320,6 @@
         for half, cols in enumerate(sides(s)):
             gain_c[s, half] = gain_turned[:, cols]
     sums[...] = jnp.zeros_like(sums)
-
-    def round_one(s, first, count, index):
-        return [
-            remote(
-                x1s.at[s, i, pl.ds(first, count)], x1r.at[s, i, pl.ds(first, count)],
-                xs1.at[index, i], xr1.at[index, i], (x_a, x_b)[i],
-            )
-            for i in range(2)
-        ]
-
-    def round_two(s, first, count, index):
-        return [
-            remote(
-                x2s.at[s, i, pl.ds(first, count)], x2r.at[s, i, pl.ds(first, count)],
-                xs2.at[index, i], xr2.at[index, i], (x_b, x_a)[i],
-            )
-            for i in range(2)
-        ]
-
-    x_sent = []
-
-    def project(s, first, count, index):
-        @pl.when(jnp.logical_not(off_diagonal))
-        def _():
-            for r in range(first, min(first + count, own)):
-                hid_got(s, r).wait_recv()
-
-        groups = slice(first, first + count)
-        weights = jnp.concatenate([wo_block(i)[...] for i in quad(s)], axis=0)
-        rows = [ctx[head, groups].reshape(count * ROWS, HEAD_DIM) for head in range(2)]
-        term = nt(rows[0], weights[:, 0:HEAD_DIM]) + nt(rows[1], weights[:, HEAD_DIM:WID])
-        for half in range(2):
-            value = term[:, half * 128 : (half + 1) * 128].reshape(count, ROWS, 128)
-            value = value + hid_in[s, groups, half].astype(F32)
-            part[s, half, groups] = value
-            x1s[s, half, groups] = value.astype(BF16)
-        for copy in round_one(s, first, count, index):
-            copy.start()
-            x_sent.append(copy)
 
     def exchange(s, first, count, index):
         groups = slice(first, first + count)
@@ -348,36 +358,29 @@
             term = nn(rows, kv_weights(s, kind)).reshape(count, ROWS, WID)
             acc[kind, groups] = term if s == 0 else acc[kind, groups] + term
 
-    def fans(s, side):
-        for i in (2 * s + 1, 2 * s + 2):
-            if i < HOPS:
-                fan_got(i, *side).wait_recv()
-
     def send_hidden(s):
         @pl.when(off_diagonal)
         def _():
             hid_copy(s).start()
 
     all_rows, early, late, end = (0, NY), (0, 2), (2, 2), STEPS - 1
-    for copy in wo_first[2:]:
-        copy.wait_recv()
     pass_on(3, ring_wo, fan_wo)
-    fans(0, fan_wo)
+    pass_on(2, ring_kv, fan_kv)
+    ctx_copy(1, 1, 1, 2, y_a).wait_recv()
+    project(0, 1, 1, 7)
     ctx_copy(0, 2, 2, 1, y_b).wait_recv()
-    project(0, *late, 0)
-    pass_on(2, ring_kv, fan_kv)
+    project(0, 2, 1, 1)
     pass_on(4, ring_wo, fan_wo)
-    ctx_copy(1, 1, 1, 2, y_a).wait_recv()
     ctx_copy(0, 0, 0, 4, y_b).wait_recv()
     ctx_copy(1, 0, 0, 5, y_a).wait_recv()
-    project(0, *early, 1)
+    project(0, 0, 1, 6)
     send_hidden(2)
     fans(1, fan_wo)
     project(1, *all_rows, 2)
     pass_on(5, ring_wo, fan_wo)
     pass_on(3, ring_kv, fan_kv)
-    exchange(0, *late, 0)
-    exchange(0, *early, 1)
+    for first, index in ((3, 0), (1, 7), (2, 1), (0, 6)):
+        exchange(0, first, 1, index)
     send_hidden(3)
     pass_on(6, ring_wo, fan_wo)
     pass_on(4, ring_kv, fan_kv)
@@ -386,8 +389,8 @@
     pass_on(7, ring_wo, fan_wo)
     exchange(1, *all_rows, 2)
     pass_on(5, ring_kv, fan_kv)
-    finish(0, *late, 0)
-    finish(0, *early, 1)
+    for first, index in ((3, 0), (1, 7), (2, 1), (0, 6)):
+        finish(0, first, 1, index)
     pass_on(8, ring_wo, fan_wo)
     fans(3, fan_wo)
     project(3, *early, 4)
@@ -459,6 +462,27 @@
     dec_col = tags(ends[1:2], base + offset, last)
     dec_allowed = (dec_col == enc_row) & (enc_row >= 0.0)
 
+    for copy in wo_first + kv_first + [dq_copy] + ctx_sent + x_sent:
+        copy.wait_send()
+
+    @pl.loop(1, HOPS)
+    def _(i):
+        hop(i + 1, *ring_wo).wait_send()
+        hop(i + 1, *ring_kv).wait_send()
+        fan(i, *fan_wo).wait_send()
+        fan(i, *fan_kv).wait_send()
+
+    @pl.when(off_diagonal)
+    def _():
+        for s in range(STEPS):
+            hid_copy(s).wait_send()
+
+    @pl.when(jnp.logical_not(off_diagonal))
+    def _():
+        for s in range(STEPS):
+            for r in range(own):
+                out_copy(s, r).wait_send()
+
     for copy in stat_copies:
         copy.wait_recv()
     square = st[own] + str_[0] + str_[1] + str_[2]
@@ -480,27 +504,8 @@
     up.start()
     cross_out[...] = jnp.concatenate([cross(slice(0, DROWS), head) for head in range(2)], axis=1)
 
-    for copy in wo_first + kv_first + [dq_copy] + ctx_sent + x_sent + y_copies + stat_copies:
+    for copy in y_copies + stat_copies:
         copy.wait_send()
-
-    @pl.loop(1, HOPS)
-    def _(i):
-        hop(i + 1, *ring_wo).wait_send()
-        hop(i + 1, *ring_kv).wait_send()
-        fan(i, *fan_wo).wait_send()
-        fan(i, *fan_kv).wait_send()
-
-    @pl.when(off_diagonal)
-    def _():
-        for s in range(STEPS):
-            hid_copy(s).wait_send()
-
-    @pl.when(jnp.logical_not(off_diagonal))
-    def _():
-        for s in range(STEPS):
-            for r in range(own):
-                out_copy(s, r).wait_send()
-
     up.wait()
     cross_out[...] = cross_out[...] + drecv[...]
 
@@ -566,8 +571,8 @@
             dma((STEPS,)), dma((STEPS, NY - 1)),
             dma((STEPS, NY - 1)), dma((STEPS,)),
             dma((6,)), dma((6,)),
-            dma((STEPS + 2, 2)), dma((STEPS + 2, 2)),
-            dma((STEPS + 2, 2)), dma((STEPS + 2, 2)),
+            dma((STEPS + 4, 2)), dma((STEPS + 4, 2)),
+            dma((STEPS + 4, 2)), dma((STEPS + 4, 2)),
             dma((6,)), dma((6,)),
             dma((NY - 1,)), dma((NY - 1,)),
         ],

time: 73.8 us -> 74.2 us (level)
  no operation moved by 1% of the time
where the time goes in v4:
time: 74.2 us; the launch traced here: 72.9 us
  Pallas kernels  69.9 us (94%)
  local copies, waits for them, and re-layouts  2.33 us (3%)
    pallas_call x1, Pallas kernels, body(): pl.pallas_call(kernel, out_shape=(jax.ShapeDtypeStruct((ROWS, FEAT), BF16...  69.9 us
    unnamed x4, local copies, waits for them, and re-layouts  2.33 us

profile of v4, /device:TPU:1, one launch (start us, length us, event | category | flops | bytes accessed | tf_op | source)
XLA Modules:
  0.0 72.9 jit_solution(16735743560612898352)
XLA Ops:
  0.6 69.9 %encoder_to_cross.1 = (bf16[128,1024]{1,0:T(8,128)(2,1)}, bf16[64,512]{1,0:T(8,128)(2,1)}) custom-call(bf16[128,1024]{1,0:T(8,128)(2,1)} %hidden.1, bf16[128,512]{1,0:T(8,128)(2,1)} %q_hbm.1, bf16[128,512]{1,0:T(8,128)(2,1)} %k_hbm.1, bf16[128,512]{1,0:T(8,128)(2,1)} %v_hbm.1, bf16[64,512]{1,0:T(8,128)(2,1)} %dq_hbm.1, bf16[32,512]{1,0:T(8,128)(2,1)} %bitcast.5, ...), custom_call_target="tpu_custom_call" | custom-call | tf_op jit(solution)/shard_map/encoder_to_cross/pallas_call | solution.py:522
  70.6 0.0 copy-start
  70.6 1.7 %copy.18 = bf16[128,1024]{1,0:T(8,128)(2,1)} copy(bf16[128,1024]{1,0:T(8,128)(2,1)} %get-tuple-element.4) | data formatting | bytes 524288
  72.3 0.0 copy-done
  72.3 0.6 copy.19
Async XLA Ops:
  70.6 1.7 %copy-start = (bf16[64,512]{1,0:T(8,128)(2,1)S(1)}, bf16[64,512]{1,0:T(8,128)(2,1)}, u32[]{:S(2)}) copy-start(bf16[64,512]{1,0:T(8,128)(2,1)} %get-tuple-element.5) | copy-start | bytes 196612

commit v5 on v3

--- a/solution.py
+++ b/solution.py
@@ -53,11 +53,11 @@
     hidden, q_hbm, k_hbm, v_hbm, dq_hbm, wo_hbm, wk_hbm, wv_hbm, gain_hbm,
     elen_hbm, dlen_hbm, order_hbm, ebound_hbm, dbound_hbm,
     enc_out, cross_out,
-    q_ref, k_ref, v_ref, gain_ref, gain_c, lens_ref, ebound, dbound,
+    q_ref, k_ref, v_ref, gain_ref, gain_c, back_c, lens_ref, ebound, dbound,
     wo, kvw, ctx, hid, hid_c, hid_in, part, x1s, x1r, x2s, x2r, res, acc, sums, out_c, out_in, out_w,
     ys, yr, st, str_, dq2, dres, drecv,
     in_sem, first_s, first_r, wo_s, wo_r, wof_s, wof_r, kv_s, kv_r, kvf_s, kvf_r,
-    dq_s, dq_r, up_s, up_r, hid_s, hid_r, out_s, out_r, ctx_s, ctx_r, xs1, xr1, xs2, xr2,
+    dq_s, dq_r, up_s, up_r, hid_s, hid_r, out_s, out_r, ctx_s, ctx_r, xs1, xr1, xs2, xr2, sum_s, sum_r,
     y_s, y_r, st_s, st_r,
 ):
     w = lax.axis_index("wide")
@@ -75,7 +75,8 @@
     z_prev = (wide(y, (z - step_dir + NZ) % NZ, c), x)
     ya, yb, y2 = y + 1 - 2 * (y % 2), NY - 1 - y, (y + 2) % NY
     y_a, y_b, y_2 = (wide(ya, z, c), x), (wide(yb, z, c), x), (wide(y2, z, c), x)
-    x_a, x_b = (w, x + 1 - 2 * (x % 2)), (w, NX - 1 - x)
+    xa, xb, x2 = x + 1 - 2 * (x % 2), NX - 1 - x, (x + 2) % NX
+    x_a, x_b = (w, xa), (w, xb)
     upper, lower = ((w + 1) % NW, x), ((w + NW - 1) % NW, x)
     adder = (wide(x, z, c), x)
     off_diagonal = x != y
@@ -270,6 +271,7 @@
     for s in range(STEPS):
         for half, cols in enumerate(sides(s)):
             gain_c[s, half] = gain_turned[:, cols]
+            back_c[s, half] = 1.0 / gain_turned[:, cols]
     sums[...] = jnp.zeros_like(sums)
 
     def round_one(s, first, count, index):
@@ -292,7 +294,7 @@
 
     x_sent = []
 
-    def project(s, first, count, index):
+    def project(s, first, count, index=None):
         @pl.when(jnp.logical_not(off_diagonal))
         def _():
             for r in range(first, min(first + count, own)):
@@ -307,9 +309,85 @@
             value = value + hid_in[s, groups, half].astype(F32)
             part[s, half, groups] = value
             x1s[s, half, groups] = value.astype(BF16)
-        for copy in round_one(s, first, count, index):
+        for copy in sum_one(s) if index is None else round_one(s, first, count, index):
             copy.start()
             x_sent.append(copy)
+
+    def sum_one(s):
+        return [
+            remote(
+                x1s.at[s, half, q], x1r.at[s, half, q], sum_s.at[s, k], sum_r.at[s, k], (x_a, x_b)[half]
+            )
+            for k, (half, q) in enumerate(((0, x2), (1, x2), (0, xa), (1, xb)))
+        ]
+
+    def sum_two(s):
+        return [
+            remote(
+                x2s.at[s, half, q], x2r.at[s, half, q], sum_s.at[s, 4 + half], sum_r.at[s, 4 + half],
+                (x_b, x_a)[half],
+            )
+            for half, q in enumerate((xb, xa))
+        ]
+
+    def spread_one(s):
+        return [
+            remote(
+                res.at[s, :, x], res.at[s, :, x], sum_s.at[s, 6 + side], sum_r.at[s, 6 + side], dev
+            )
+            for side, dev in enumerate((x_a, x_b))
+        ]
+
+    def spread_two(s):
+        return [
+            remote(
+                res.at[s, half, q], res.at[s, half, q], sum_s.at[s, 8 + half], sum_r.at[s, 8 + half],
+                (x_b, x_a)[half],
+            )
+            for half, q in enumerate((xa, xb))
+        ]
+
+    def send(copy):
+        copy.start()
+        x_sent.append(copy)
+
+    def relay_sum(s):
+        for half, q in enumerate((xb, xa)):
+            sum_one(s)[half].wait_recv()
+            total = part[s, half, q] + x1r[s, half, q].astype(F32)
+            x2s[s, half, q] = total.astype(BF16)
+            send(sum_two(s)[half])
+
+    def own_sum(s):
+        for half in range(2):
+            sum_one(s)[2 + half].wait_recv()
+            sum_two(s)[half].wait_recv()
+            total = part[s, half, x] + x1r[s, half, x].astype(F32) + x2r[s, half, x].astype(F32)
+            res[s, half, x] = (total * gain_c[s, half, 0:1, :]).astype(BF16)
+        for copy in spread_one(s):
+            send(copy)
+
+    def relay_spread(s):
+        for side in range(2):
+            spread_one(s)[side].wait_recv()
+            send(spread_two(s)[side])
+
+    def gathered(s):
+        for copy in spread_two(s):
+            copy.wait_recv()
+        for half in range(2):
+            total = res[s, half].astype(F32) * back_c[s, half, 0:1, :]
+            sums[...] += total * total
+            out_c[s, :, half] = total.astype(BF16)
+        go_home(s, 0, NY)
+
+    def go_home(s, first, count):
+        @pl.when(jnp.logical_not(off_diagonal))
+        def _():
+            for r in range(first, min(first + count, own)):
+                out_copy(s, r).start()
+            if first + count > own:
+                out_in[s] = out_c[s, own]
 
     def exchange(s, first, count, index):
         groups = slice(first, first + count)
@@ -328,22 +406,17 @@
             copy.wait_recv()
             total = part[s, half, groups] + x2r[s, half, groups].astype(F32)
             sums[groups] += total * total
-            res[s, groups, :, half * 128 : (half + 1) * 128] = (total * gain_c[s, half, 0:1, :]).astype(BF16)
+            res[s, half, groups] = (total * gain_c[s, half, 0:1, :]).astype(BF16)
             out_c[s, groups, half] = total.astype(BF16)
-
-        @pl.when(jnp.logical_not(off_diagonal))
-        def _():
-            for r in range(first, min(first + count, own)):
-                out_copy(s, r).start()
-            if first + count > own:
-                out_in[s] = out_c[s, own]
+        go_home(s, first, count)
 
     def kv_weights(s, kind):
         return jnp.concatenate([kvw[number(i), kind] for i in quad(s)], axis=0)
 
     def accumulate(s, first, count):
         groups = slice(first, first + count)
-        rows = res[s, groups].reshape(count * ROWS, 4 * BLK)
+        rows = [res[s, half, groups].reshape(count * ROWS, 2 * BLK) for half in range(2)]
+        rows = jnp.concatenate(rows, axis=1)
         for kind in range(2):
             term = nn(rows, kv_weights(s, kind)).reshape(count, ROWS, WID)
             acc[kind, groups] = term if s == 0 else acc[kind, groups] + term
@@ -364,48 +437,51 @@
     pass_on(3, ring_wo, fan_wo)
     fans(0, fan_wo)
     ctx_copy(0, 2, 2, 1, y_b).wait_recv()
-    project(0, *late, 0)
+    ctx_copy(1, 1, 1, 2, y_a).wait_recv()
     pass_on(2, ring_kv, fan_kv)
-    pass_on(4, ring_wo, fan_wo)
-    ctx_copy(1, 1, 1, 2, y_a).wait_recv()
     ctx_copy(0, 0, 0, 4, y_b).wait_recv()
     ctx_copy(1, 0, 0, 5, y_a).wait_recv()
-    project(0, *early, 1)
+    project(0, *all_rows)
     send_hidden(2)
+    pass_on(4, ring_wo, fan_wo)
     fans(1, fan_wo)
-    project(1, *all_rows, 2)
+    project(1, *all_rows)
     pass_on(5, ring_wo, fan_wo)
     pass_on(3, ring_kv, fan_kv)
-    exchange(0, *late, 0)
-    exchange(0, *early, 1)
+    relay_sum(0)
     send_hidden(3)
     pass_on(6, ring_wo, fan_wo)
+    own_sum(0)
     pass_on(4, ring_kv, fan_kv)
+    relay_sum(1)
     fans(2, fan_wo)
-    project(2, *all_rows, 3)
+    project(2, *all_rows)
     pass_on(7, ring_wo, fan_wo)
-    exchange(1, *all_rows, 2)
+    relay_spread(0)
+    own_sum(1)
     pass_on(5, ring_kv, fan_kv)
-    finish(0, *late, 0)
-    finish(0, *early, 1)
+    relay_sum(2)
     pass_on(8, ring_wo, fan_wo)
+    gathered(0)
     fans(3, fan_wo)
-    project(3, *early, 4)
-    project(3, *late, 5)
+    project(3, *early, 0)
+    project(3, *late, 1)
     pass_on(6, ring_kv, fan_kv)
+    relay_spread(1)
+    own_sum(2)
     for copy in kv_first[2:]:
         copy.wait_recv()
     fans(0, fan_kv)
     accumulate(0, *all_rows)
-    exchange(2, *all_rows, 3)
     pass_on(7, ring_kv, fan_kv)
-    finish(1, *all_rows, 2)
+    gathered(1)
+    exchange(3, *early, 0)
+    exchange(3, *late, 1)
+    relay_spread(2)
     fans(1, fan_kv)
     accumulate(1, *all_rows)
-    exchange(3, *early, 4)
-    exchange(3, *late, 5)
     pass_on(8, ring_kv, fan_kv)
-    finish(2, *all_rows, 3)
+    gathered(2)
     fans(2, fan_kv)
     accumulate(2, *all_rows)
     fans(3, fan_kv)
@@ -419,12 +495,12 @@
     def y_read(i):
         return yr[i].astype(F32)
 
-    finish(end, *early, 4)
+    finish(end, *early, 0)
     accumulate(end, *early)
     y_send(0, acc[0, 0])
     y_send(1, acc[1, 0])
     y_send(2, acc[0, 1])
-    finish(end, *late, 5)
+    finish(end, *late, 1)
     accumulate(end, *late)
     y_send(3, acc[1, 2])
     y_copies[1].wait_recv()
@@ -528,6 +604,7 @@
             pltpu.VMEM((ROWS, WID), BF16),
             pltpu.VMEM(gain.shape, F32),
             pltpu.VMEM((STEPS, 2, 8, 128), F32),
+            pltpu.VMEM((STEPS, 2, 8, 128), F32),
             pltpu.VMEM((3, 1, 256), jnp.int32),
             pltpu.SMEM(enc_bounds.shape, jnp.int32),
             pltpu.SMEM(dec_bounds.shape, jnp.int32),
@@ -542,7 +619,7 @@
             pltpu.VMEM((STEPS, 2, NY) + square, BF16),
             pltpu.VMEM((STEPS, 2, NY) + square, BF16),
             pltpu.VMEM((STEPS, 2, NY) + square, BF16),
-            pltpu.VMEM((STEPS, NY, ROWS, 4 * BLK), BF16),
+            pltpu.VMEM((STEPS, 2, NY) + square, BF16),
             pltpu.VMEM((2, NY, ROWS, WID), F32),
             pltpu.VMEM((NY,) + square, F32),
             pltpu.VMEM((STEPS, NY, 2) + square, BF16),
@@ -566,8 +643,9 @@
             dma((STEPS,)), dma((STEPS, NY - 1)),
             dma((STEPS, NY - 1)), dma((STEPS,)),
             dma((6,)), dma((6,)),
-            dma((STEPS + 2, 2)), dma((STEPS + 2, 2)),
-            dma((STEPS + 2, 2)), dma((STEPS + 2, 2)),
+            dma((2, 2)), dma((2, 2)),
+            dma((2, 2)), dma((2, 2)),
+            dma((STEPS - 1, 10)), dma((STEPS - 1, 10)),
             dma((6,)), dma((6,)),
             dma((NY - 1,)), dma((NY - 1,)),
         ],

time: 73.8 us -> 75.2 us (1.019); the launches traced: 72.8 us -> 75 us
  Pallas kernels: 69.8 us -> 72 us
    pallas_call x1, Pallas kernels: 69.8 us -> 72 us  [body(): pl.pallas_call(kernel, out_shape=(jax.ShapeDtypeStruct((ROWS, FEAT), BF16...]
where the time goes in v5:
time: 75.2 us; the launch traced here: 75 us
  Pallas kernels  72 us (96%)
  local copies, waits for them, and re-layouts  2.33 us (3%)
    pallas_call x1, Pallas kernels, body(): pl.pallas_call(kernel, out_shape=(jax.ShapeDtypeStruct((ROWS, FEAT), BF16...  72 us
    unnamed x4, local copies, waits for them, and re-layouts  2.33 us

profile of v5, /device:TPU:1, one launch (start us, length us, event | category | flops | bytes accessed | tf_op | source)
XLA Modules:
  0.0 75.0 jit_solution(14919946039884456919)
XLA Ops:
  0.6 72.0 %encoder_to_cross.1 = (bf16[128,1024]{1,0:T(8,128)(2,1)}, bf16[64,512]{1,0:T(8,128)(2,1)}) custom-call(bf16[128,1024]{1,0:T(8,128)(2,1)} %hidden.1, bf16[128,512]{1,0:T(8,128)(2,1)} %q_hbm.1, bf16[128,512]{1,0:T(8,128)(2,1)} %k_hbm.1, bf16[128,512]{1,0:T(8,128)(2,1)} %v_hbm.1, bf16[64,512]{1,0:T(8,128)(2,1)} %dq_hbm.1, bf16[32,512]{1,0:T(8,128)(2,1)} %bitcast.5, ...), custom_call_target="tpu_custom_call" | custom-call | tf_op jit(solution)/shard_map/encoder_to_cross/pallas_call | solution.py:593
  72.7 0.0 copy-start
  72.7 1.7 %copy.18 = bf16[128,1024]{1,0:T(8,128)(2,1)} copy(bf16[128,1024]{1,0:T(8,128)(2,1)} %get-tuple-element.4) | data formatting | bytes 524288
  74.4 0.0 copy-done
  74.4 0.6 copy.19
Async XLA Ops:
  72.7 1.7 %copy-start = (bf16[64,512]{1,0:T(8,128)(2,1)S(1)}, bf16[64,512]{1,0:T(8,128)(2,1)}, u32[]{:S(2)}) copy-start(bf16[64,512]{1,0:T(8,128)(2,1)} %get-tuple-element.5) | copy-start | bytes 196612

commit v6 on v3

--- a/solution.py
+++ b/solution.py
@@ -56,7 +56,7 @@
     q_ref, k_ref, v_ref, gain_ref, gain_c, lens_ref, ebound, dbound,
     wo, kvw, ctx, hid, hid_c, hid_in, part, x1s, x1r, x2s, x2r, res, acc, sums, out_c, out_in, out_w,
     ys, yr, st, str_, dq2, dres, drecv,
-    in_sem, first_s, first_r, wo_s, wo_r, wof_s, wof_r, kv_s, kv_r, kvf_s, kvf_r,
+    in_sem, first_s, first_r, wo_s, wo_r, wof_r, kv_s, kv_r, kvf_r,
     dq_s, dq_r, up_s, up_r, hid_s, hid_r, out_s, out_r, ctx_s, ctx_r, xs1, xr1, xs2, xr2,
     y_s, y_r, st_s, st_r,
 ):
@@ -98,9 +98,9 @@
         pl.semaphore_signal(barrier, inc=1, device_id=dev, device_id_type=MESH)
 
     piece = cols_of(c, PIECE)
-    mine = pl.ds(pl.multiple_of(z * BLK + c * PIECE, PIECE), PIECE)
+    mine = piece
     pairs = (
-        (wk_hbm, kvw.at[z, 0, piece]), (wv_hbm, kvw.at[z, 1, piece]),
+        (wk_hbm, kvw.at[0, 0, piece]), (wv_hbm, kvw.at[0, 1, piece]),
         (hidden, hid.at[:, pl.ds(0, FEAT)]), (hidden, hid.at[:, pl.ds(FEAT, FEAT)]), (wo_hbm, wo.at[mine]),
         (elen_hbm, lens_ref.at[0]), (dlen_hbm, lens_ref.at[1]), (order_hbm, lens_ref.at[2]),
         (ebound_hbm, ebound), (dbound_hbm, dbound),
@@ -113,13 +113,23 @@
 
     pl.semaphore_wait(barrier, len(greet))
 
-    around = (z_next, cross, sib)
+    def out_at(i):
+        return jnp.where(c == 0, NZ - i, i)
+
+    def in_at(i):
+        return jnp.where(c == 0, i, NZ - i)
+
+    def rows_at(i, offset, count):
+        return pl.ds(pl.multiple_of(i * BLK + offset, PIECE), count)
+
+    around = ((z_next, out_at(1)), (cross, in_at(1)), (sib, 0))
     wo_first = [
-        remote(wo_hbm, wo.at[mine], first_s.at[i], first_r.at[i], dev) for i, dev in enumerate(around)
+        remote(wo_hbm, wo.at[rows_at(to, c * PIECE, PIECE)], wo_s, first_r.at[i], dev)
+        for i, (dev, to) in enumerate(around)
     ]
     kv_first = [
-        remote(kvw.at[z, :, piece], kvw.at[z, :, piece], first_s.at[3 + i], first_r.at[3 + i], dev)
-        for i, dev in enumerate(around)
+        remote(kvw.at[0, :, piece], kvw.at[to, :, piece], first_s, first_r.at[3 + i], dev)
+        for i, (dev, to) in enumerate(around)
     ]
     for copy in wo_first:
         copy.start()
@@ -138,13 +148,13 @@
         return slice(s * 128, (s + 1) * 128), slice((LANES - 1 - s) * 128, (LANES - s) * 128)
 
     def hid_copy(s):
-        return remote(hid_c.at[s], hid_in.at[s, relation], hid_s.at[s], hid_r.at[s, relation], adder)
+        return remote(hid_c.at[s], hid_in.at[s, relation], hid_s, hid_r.at[s, relation], adder)
 
     def hid_got(s, r):
-        return remote(hid_in.at[s, r], hid_in.at[s, r], hid_s.at[s], hid_r.at[s, r], adder)
+        return remote(hid_in.at[s, r], hid_in.at[s, r], hid_s, hid_r.at[s, r], adder)
 
     def out_copy(s, r):
-        return remote(out_c.at[s, r], out_in.at[s], out_s.at[s, r], out_r.at[s], near[r])
+        return remote(out_c.at[s, r], out_in.at[s], out_s, out_r.at[s], near[r])
 
     for load in loads[2:4]:
         load.wait()
@@ -187,76 +197,61 @@
     enc_row = jnp.sum(jnp.where(diag, enc_col, 0.0), axis=0, keepdims=True)
     enc_allowed = (enc_col == enc_row) & (enc_row >= 0.0)
 
-    def number(i):
-        return (i + 2 * NZ) % NZ
-
-    def wo_block(i):
-        return wo.at[cols_of(number(i), BLK)]
-
-    def kv_block(i):
-        return kvw.at[number(i)]
-
-    def hop(i, buffer, ss, rs):
-        at = buffer(z - step_dir * (i - 1))
-        return remote(at, at, ss.at[i - 1], rs.at[i - 1], z_next)
-
-    def got(i, buffer, ss, rs):
-        at = buffer(z - step_dir * i)
-        return remote(at, at, ss.at[i - 1], rs.at[i - 1], z_next)
-
-    def fan(i, buffer, ss, rs):
-        at = buffer(z - step_dir * i)
-        return remote(at, at, ss.at[i - 1], rs.at[i - 1], sib)
-
-    def fan_got(i, buffer, ss, rs):
-        at = buffer(z + step_dir * i)
-        return remote(at, at, ss.at[i - 1], rs.at[i - 1], sib)
-
-    ring_wo, fan_wo = (wo_block, wo_s, wo_r), (wo_block, wof_s, wof_r)
-    ring_kv, fan_kv = (kv_block, kv_s, kv_r), (kv_block, kvf_s, kvf_r)
-
-    def forward(i, ring, side):
+    def wo_blocks(i, count):
+        return wo.at[rows_at(i, 0, count * BLK)]
+
+    def kv_blocks(i, count):
+        return kvw.at[pl.ds(i, count)]
+
+    def hop(i, blocks, ss, rs, _):
+        return remote(blocks(out_at(i - 1), 1), blocks(out_at(i), 1), ss, rs.at[i - 1], z_next)
+
+    def fan(k, blocks, ss, _, rs, arrives=False):
+        count = min(2, HOPS - 1 - 2 * k)
+        low = NZ - 2 * k - count if count == 2 else NZ - 2 * k - 1
+        start = jnp.where(c == (1 if arrives else 0), low, 2 * k + 1)
+        at = blocks(start, count)
+        return remote(at, at, ss, rs.at[k], sib)
+
+    ring_wo = (wo_blocks, wo_s, wo_r, wof_r)
+    ring_kv = (kv_blocks, kv_s, kv_r, kvf_r)
+
+    def forward(i, ring):
         hop(i + 1, *ring).start()
-        fan(i, *side).start()
-
-    def pass_on(i, ring, side):
-        got(i, *ring).wait_recv()
-
-        @pl.when(i < HOPS)
-        def _():
-            forward(i, ring, side)
-
-    def quad(s):
-        return z + 2 * s, z + 2 * s + 1, z - 2 * s - 2, z - 2 * s - 1
+        if i % 2 == 0 or i == HOPS - 1:
+            fan((i - 1) // 2, *ring).start()
+
+    def pass_on(i, ring):
+        hop(i, *ring).wait_recv()
+        if i < HOPS:
+            forward(i, ring)
 
     def ctx_copy(head, src, dst, index, dev):
-        return remote(ctx.at[head, src], ctx.at[head, dst], ctx_s.at[index], ctx_r.at[index], dev)
+        return remote(ctx.at[head, src], ctx.at[head, dst], ctx_s, ctx_r.at[index], dev)
 
     for copy in wo_first[:2]:
         copy.wait_recv()
-    forward(1, ring_wo, fan_wo)
+    forward(1, ring_wo)
     for load in loads[10:]:
         load.wait()
     for head in range(2):
         cols = slice(head * HEAD_DIM, (head + 1) * HEAD_DIM)
         ctx[head, own] = attend(q_ref[:, cols], k_ref[:, cols], v_ref[:, cols], enc_allowed)
-    ctx_sent = [
+    ctx_first = [
         ctx_copy(0, own, 1, 0, y_a), ctx_copy(1, own, 2, 3, y_b),
         ctx_copy(1, own, 1, 2, y_a), ctx_copy(0, own, 2, 1, y_b),
     ]
-    for copy in ctx_sent:
+    for copy in ctx_first:
         copy.start()
     for copy in kv_first[:2]:
         copy.wait_recv()
-    forward(1, ring_kv, fan_kv)
-    pass_on(2, ring_wo, fan_wo)
+    forward(1, ring_kv)
+    pass_on(2, ring_wo)
 
     ctx_copy(0, 1, 1, 0, y_a).wait_recv()
-    ctx_sent.append(ctx_copy(0, 1, 0, 4, y_b))
-    ctx_sent[-1].start()
+    ctx_copy(0, 1, 0, 4, y_b).start()
     ctx_copy(1, 2, 2, 3, y_b).wait_recv()
-    ctx_sent.append(ctx_copy(1, 2, 0, 5, y_a))
-    ctx_sent[-1].start()
+    ctx_copy(1, 2, 0, 5, y_a).start()
 
     @pl.when(off_diagonal)
     def _():
@@ -276,7 +271,7 @@
         return [
             remote(
                 x1s.at[s, i, pl.ds(first, count)], x1r.at[s, i, pl.ds(first, count)],
-                xs1.at[index, i], xr1.at[index, i], (x_a, x_b)[i],
+                xs1, xr1.at[index, i], (x_a, x_b)[i],
             )
             for i in range(2)
         ]
@@ -285,12 +280,10 @@
         return [
             remote(
                 x2s.at[s, i, pl.ds(first, count)], x2r.at[s, i, pl.ds(first, count)],
-                xs2.at[index, i], xr2.at[index, i], (x_b, x_a)[i],
+                xs2, xr2.at[index, i], (x_b, x_a)[i],
             )
             for i in range(2)
         ]
-
-    x_sent = []
 
     def project(s, first, count, index):
         @pl.when(jnp.logical_not(off_diagonal))
@@ -299,7 +292,7 @@
                 hid_got(s, r).wait_recv()
 
         groups = slice(first, first + count)
-        weights = jnp.concatenate([wo_block(i)[...] for i in quad(s)], axis=0)
+        weights = jnp.concatenate([wo[cols, :] for cols in sides(s)], axis=0)
         rows = [ctx[head, groups].reshape(count * ROWS, HEAD_DIM) for head in range(2)]
         term = nt(rows[0], weights[:, 0:HEAD_DIM]) + nt(rows[1], weights[:, HEAD_DIM:WID])
         for half in range(2):
@@ -309,7 +302,6 @@
             x1s[s, half, groups] = value.astype(BF16)
         for copy in round_one(s, first, count, index):
             copy.start()
-            x_sent.append(copy)
 
     def exchange(s, first, count, index):
         groups = slice(first, first + count)
@@ -320,7 +312,6 @@
             x2s[s, half, groups] = total.astype(BF16)
             copy = round_two(s, first, count, index)[half]
             copy.start()
-            x_sent.append(copy)
 
     def finish(s, first, count, index):
         groups = slice(first, first + count)
@@ -339,7 +330,8 @@
                 out_in[s] = out_c[s, own]
 
     def kv_weights(s, kind):
-        return jnp.concatenate([kvw[number(i), kind] for i in quad(s)], axis=0)
+        quad = (2 * s, 2 * s + 1, NZ - 2 - 2 * s, NZ - 1 - 2 * s)
+        return jnp.concatenate([kvw[i, kind] for i in quad], axis=0)
 
     def accumulate(s, first, count):
         groups = slice(first, first + count)
@@ -348,10 +340,8 @@
             term = nn(rows, kv_weights(s, kind)).reshape(count, ROWS, WID)
             acc[kind, groups] = term if s == 0 else acc[kind, groups] + term
 
-    def fans(s, side):
-        for i in (2 * s + 1, 2 * s + 2):
-            if i < HOPS:
-                fan_got(i, *side).wait_recv()
+    def fans(s, ring):
+        fan(s, *ring, arrives=True).wait_recv()
 
     def send_hidden(s):
         @pl.when(off_diagonal)
@@ -361,56 +351,56 @@
     all_rows, early, late, end = (0, NY), (0, 2), (2, 2), STEPS - 1
     for copy in wo_first[2:]:
         copy.wait_recv()
-    pass_on(3, ring_wo, fan_wo)
-    fans(0, fan_wo)
+    pass_on(3, ring_wo)
+    fans(0, ring_wo)
     ctx_copy(0, 2, 2, 1, y_b).wait_recv()
     project(0, *late, 0)
-    pass_on(2, ring_kv, fan_kv)
-    pass_on(4, ring_wo, fan_wo)
+    pass_on(2, ring_kv)
+    pass_on(4, ring_wo)
     ctx_copy(1, 1, 1, 2, y_a).wait_recv()
     ctx_copy(0, 0, 0, 4, y_b).wait_recv()
     ctx_copy(1, 0, 0, 5, y_a).wait_recv()
     project(0, *early, 1)
     send_hidden(2)
-    fans(1, fan_wo)
+    fans(1, ring_wo)
     project(1, *all_rows, 2)
-    pass_on(5, ring_wo, fan_wo)
-    pass_on(3, ring_kv, fan_kv)
+    pass_on(5, ring_wo)
+    pass_on(3, ring_kv)
     exchange(0, *late, 0)
     exchange(0, *early, 1)
     send_hidden(3)
-    pass_on(6, ring_wo, fan_wo)
-    pass_on(4, ring_kv, fan_kv)
-    fans(2, fan_wo)
+    pass_on(6, ring_wo)
+    pass_on(4, ring_kv)
+    fans(2, ring_wo)
     project(2, *all_rows, 3)
-    pass_on(7, ring_wo, fan_wo)
+    pass_on(7, ring_wo)
     exchange(1, *all_rows, 2)
-    pass_on(5, ring_kv, fan_kv)
+    pass_on(5, ring_kv)
     finish(0, *late, 0)
     finish(0, *early, 1)
-    pass_on(8, ring_wo, fan_wo)
-    fans(3, fan_wo)
+    pass_on(8, ring_wo)
+    fans(3, ring_wo)
     project(3, *early, 4)
     project(3, *late, 5)
-    pass_on(6, ring_kv, fan_kv)
+    pass_on(6, ring_kv)
     for copy in kv_first[2:]:
         copy.wait_recv()
-    fans(0, fan_kv)
+    fans(0, ring_kv)
     accumulate(0, *all_rows)
     exchange(2, *all_rows, 3)
-    pass_on(7, ring_kv, fan_kv)
+    pass_on(7, ring_kv)
     finish(1, *all_rows, 2)
-    fans(1, fan_kv)
+    fans(1, ring_kv)
     accumulate(1, *all_rows)
     exchange(3, *early, 4)
     exchange(3, *late, 5)
-    pass_on(8, ring_kv, fan_kv)
+    pass_on(8, ring_kv)
     finish(2, *all_rows, 3)
-    fans(2, fan_kv)
+    fans(2, ring_kv)
     accumulate(2, *all_rows)
-    fans(3, fan_kv)
-
-    y_copies = [remote(ys.at[i], yr.at[i], y_s.at[i], y_r.at[i], (y_a, y_b)[i % 2]) for i in range(6)]
+    fans(3, ring_kv)
+
+    y_copies = [remote(ys.at[i], yr.at[i], y_s, y_r.at[i], (y_a, y_b)[i % 2]) for i in range(6)]
 
     def y_send(i, value):
         ys[i] = value.astype(BF16)
@@ -435,7 +425,7 @@
     columns = jnp.sum(sums[...], axis=2, keepdims=True)
     squares = jnp.sum(jnp.where(diag[None], columns, 0.0), axis=1, keepdims=True)
     st[...] = jnp.broadcast_to(squares, (NY, 8, ROWS))
-    stat_copies = [remote(st.at[r], str_.at[r], st_s.at[r], st_r.at[r], near[r]) for r in range(own)]
+    stat_copies = [remote(st.at[r], str_.at[r], st_s, st_r.at[r], near[r]) for r in range(own)]
     for copy in stat_copies:
         copy.start()
 
@@ -480,26 +470,26 @@
     up.start()
     cross_out[...] = jnp.concatenate([cross(slice(0, DROWS), head) for head in range(2)], axis=1)
 
-    for copy in wo_first + kv_first + [dq_copy] + ctx_sent + x_sent + y_copies + stat_copies:
-        copy.wait_send()
-
-    @pl.loop(1, HOPS)
-    def _(i):
-        hop(i + 1, *ring_wo).wait_send()
-        hop(i + 1, *ring_kv).wait_send()
-        fan(i, *fan_wo).wait_send()
-        fan(i, *fan_kv).wait_send()
+    def left(sent, sem):
+        remote(sent, sent, sem, up_r, sib).wait_send()
+
+    left(wo.at[pl.ds(0, 14 * BLK + 3 * PIECE)], wo_s)
+    left(kvw.at[pl.ds(0, 14)], kv_s)
+    left(kvw.at[pl.ds(0, 3), 0], first_s)
+    left(ctx.at[:, pl.ds(0, 3)], ctx_s)
+    left(x1s, xs1)
+    left(x2s, xs2)
+    left(ys, y_s)
+    left(st.at[pl.ds(0, 3)], st_s)
+    dq_copy.wait_send()
 
     @pl.when(off_diagonal)
     def _():
-        for s in range(STEPS):
-            hid_copy(s).wait_send()
+        left(hid_c, hid_s)
 
     @pl.when(jnp.logical_not(off_diagonal))
     def _():
-        for s in range(STEPS):
-            for r in range(own):
-                out_copy(s, r).wait_send()
+        left(out_c.at[pl.ds(0, 3)], out_s)
 
     up.wait()
     cross_out[...] = cross_out[...] + drecv[...]
@@ -556,20 +546,18 @@
             pltpu.VMEM((DROWS, WID), BF16),
             pltpu.VMEM((DROWS, WID), BF16),
             dma((15,)),
-            dma((6,)), dma((6,)),
-            dma((HOPS,)), dma((HOPS,)),
-            dma((HOPS,)), dma((HOPS,)),
-            dma((HOPS,)), dma((HOPS,)),
-            dma((HOPS,)), dma((HOPS,)),
+            dma, dma((6,)),
+            dma, dma((HOPS,)), dma((STEPS,)),
+            dma, dma((HOPS,)), dma((STEPS,)),
             dma, dma,
             dma, dma,
-            dma((STEPS,)), dma((STEPS, NY - 1)),
-            dma((STEPS, NY - 1)), dma((STEPS,)),
-            dma((6,)), dma((6,)),
-            dma((STEPS + 2, 2)), dma((STEPS + 2, 2)),
-            dma((STEPS + 2, 2)), dma((STEPS + 2, 2)),
-            dma((6,)), dma((6,)),
-            dma((NY - 1,)), dma((NY - 1,)),
+            dma, dma((STEPS, NY - 1)),
+            dma, dma((STEPS,)),
+            dma, dma((6,)),
+            dma, dma((STEPS + 2, 2)),
+            dma, dma((STEPS + 2, 2)),
+            dma, dma((6,)),
+            dma, dma((NY - 1,)),
         ],
         compiler_params=pltpu.CompilerParams(
             collective_id=0, has_side_effects=True, vmem_limit_bytes=VMEM_LIMIT

time: 73.8 us -> 73.2 us (level)
  Pallas kernels: 69.8 us -> 69 us
    pallas_call x1, Pallas kernels: 69.8 us -> 69 us  [body(): pl.pallas_call(kernel, out_shape=(jax.ShapeDtypeStruct((ROWS, FEAT), BF16...]
where the time goes in v6:
time: 73.2 us; the launch traced here: 72 us
  Pallas kernels  69 us (94%)
  local copies, waits for them, and re-layouts  2.33 us (3%)
    pallas_call x1, Pallas kernels, body(): pl.pallas_call(kernel, out_shape=(jax.ShapeDtypeStruct((ROWS, FEAT), BF16...  69 us
    unnamed x4, local copies, waits for them, and re-layouts  2.33 us

profile of v6, /device:TPU:1, one launch (start us, length us, event | category | flops | bytes accessed | tf_op | source)
XLA Modules:
  0.0 72.0 jit_solution(17082108455278685288)
XLA Ops:
  0.6 69.0 %encoder_to_cross.1 = (bf16[128,1024]{1,0:T(8,128)(2,1)}, bf16[64,512]{1,0:T(8,128)(2,1)}) custom-call(bf16[128,1024]{1,0:T(8,128)(2,1)} %hidden.1, bf16[128,512]{1,0:T(8,128)(2,1)} %q_hbm.1, bf16[128,512]{1,0:T(8,128)(2,1)} %k_hbm.1, bf16[128,512]{1,0:T(8,128)(2,1)} %v_hbm.1, bf16[64,512]{1,0:T(8,128)(2,1)} %dq_hbm.1, bf16[32,512]{1,0:T(8,128)(2,1)} %bitcast.5, ...), custom_call_target="tpu_custom_call" | custom-call | tf_op jit(solution)/shard_map/encoder_to_cross/pallas_call | solution.py:507
  69.6 0.0 copy-start
  69.6 1.7 %copy.18 = bf16[128,1024]{1,0:T(8,128)(2,1)} copy(bf16[128,1024]{1,0:T(8,128)(2,1)} %get-tuple-element.4) | data formatting | bytes 524288
  71.3 0.0 copy-done
  71.3 0.6 copy.19
Async XLA Ops:
  69.6 1.7 %copy-start = (bf16[64,512]{1,0:T(8,128)(2,1)S(1)}, bf16[64,512]{1,0:T(8,128)(2,1)}, u32[]{:S(2)}) copy-start(bf16[64,512]{1,0:T(8,128)(2,1)} %get-tuple-element.5) | copy-start | bytes 196612

commit v7 on v6

--- a/solution.py
+++ b/solution.py
@@ -232,6 +232,9 @@
     for copy in wo_first[:2]:
         copy.wait_recv()
     forward(1, ring_wo)
+    for copy in kv_first[:2]:
+        copy.wait_recv()
+    forward(1, ring_kv)
     for load in loads[10:]:
         load.wait()
     for head in range(2):
@@ -243,9 +246,6 @@
     ]
     for copy in ctx_first:
         copy.start()
-    for copy in kv_first[:2]:
-        copy.wait_recv()
-    forward(1, ring_kv)
     pass_on(2, ring_wo)
 
     ctx_copy(0, 1, 1, 0, y_a).wait_recv()
@@ -349,52 +349,50 @@
             hid_copy(s).start()
 
     all_rows, early, late, end = (0, NY), (0, 2), (2, 2), STEPS - 1
-    for copy in wo_first[2:]:
+    for copy in wo_first[2:] + kv_first[2:]:
         copy.wait_recv()
+    pass_on(2, ring_kv)
     pass_on(3, ring_wo)
     fans(0, ring_wo)
     ctx_copy(0, 2, 2, 1, y_b).wait_recv()
     project(0, *late, 0)
-    pass_on(2, ring_kv)
-    pass_on(4, ring_wo)
     ctx_copy(1, 1, 1, 2, y_a).wait_recv()
     ctx_copy(0, 0, 0, 4, y_b).wait_recv()
     ctx_copy(1, 0, 0, 5, y_a).wait_recv()
     project(0, *early, 1)
     send_hidden(2)
+    pass_on(3, ring_kv)
+    pass_on(4, ring_wo)
     fans(1, ring_wo)
     project(1, *all_rows, 2)
     pass_on(5, ring_wo)
-    pass_on(3, ring_kv)
+    pass_on(4, ring_kv)
     exchange(0, *late, 0)
     exchange(0, *early, 1)
     send_hidden(3)
     pass_on(6, ring_wo)
-    pass_on(4, ring_kv)
     fans(2, ring_wo)
     project(2, *all_rows, 3)
+    pass_on(5, ring_kv)
     pass_on(7, ring_wo)
     exchange(1, *all_rows, 2)
-    pass_on(5, ring_kv)
     finish(0, *late, 0)
     finish(0, *early, 1)
     pass_on(8, ring_wo)
+    pass_on(6, ring_kv)
     fans(3, ring_wo)
     project(3, *early, 4)
     project(3, *late, 5)
-    pass_on(6, ring_kv)
-    for copy in kv_first[2:]:
-        copy.wait_recv()
-    fans(0, ring_kv)
-    accumulate(0, *all_rows)
     exchange(2, *all_rows, 3)
     pass_on(7, ring_kv)
     finish(1, *all_rows, 2)
-    fans(1, ring_kv)
-    accumulate(1, *all_rows)
+    fans(0, ring_kv)
+    accumulate(0, *all_rows)
     exchange(3, *early, 4)
     exchange(3, *late, 5)
     pass_on(8, ring_kv)
+    fans(1, ring_kv)
+    accumulate(1, *all_rows)
     finish(2, *all_rows, 3)
     fans(2, ring_kv)
     accumulate(2, *all_rows)

time: 73.2 us -> 72.3 us (0.988); the launches traced: 72 us -> 72.1 us
  no operation moved by 1% of the time
where the time goes in v7:
time: 72.3 us; the launch traced here: 72.1 us
  Pallas kernels  69.1 us (96%)
  local copies, waits for them, and re-layouts  2.33 us (3%)
    pallas_call x1, Pallas kernels, body(): pl.pallas_call(kernel, out_shape=(jax.ShapeDtypeStruct((ROWS, FEAT), BF16...  69.1 us
    unnamed x4, local copies, waits for them, and re-layouts  2.33 us

profile of v7, /device:TPU:1, one launch (start us, length us, event | category | flops | bytes accessed | tf_op | source)
XLA Modules:
  0.0 72.1 jit_solution(15212283946307619083)
XLA Ops:
  0.6 69.1 %encoder_to_cross.1 = (bf16[128,1024]{1,0:T(8,128)(2,1)}, bf16[64,512]{1,0:T(8,128)(2,1)}) custom-call(bf16[128,1024]{1,0:T(8,128)(2,1)} %hidden.1, bf16[128,512]{1,0:T(8,128)(2,1)} %q_hbm.1, bf16[128,512]{1,0:T(8,128)(2,1)} %k_hbm.1, bf16[128,512]{1,0:T(8,128)(2,1)} %v_hbm.1, bf16[64,512]{1,0:T(8,128)(2,1)} %dq_hbm.1, bf16[32,512]{1,0:T(8,128)(2,1)} %bitcast.5, ...), custom_call_target="tpu_custom_call" | custom-call | tf_op jit(solution)/shard_map/encoder_to_cross/pallas_call | solution.py:505
  69.7 0.0 copy-start
  69.7 1.7 %copy.18 = bf16[128,1024]{1,0:T(8,128)(2,1)} copy(bf16[128,1024]{1,0:T(8,128)(2,1)} %get-tuple-element.4) | data formatting | bytes 524288
  71.4 0.0 copy-done
  71.4 0.6 copy.19
Async XLA Ops:
  69.7 1.7 %copy-start = (bf16[64,512]{1,0:T(8,128)(2,1)S(1)}, bf16[64,512]{1,0:T(8,128)(2,1)}, u32[]{:S(2)}) copy-start(bf16[64,512]{1,0:T(8,128)(2,1)} %get-tuple-element.5) | copy-start | bytes 196612

commit v8 on v7

--- a/solution.py
+++ b/solution.py
@@ -54,7 +54,7 @@
     elen_hbm, dlen_hbm, order_hbm, ebound_hbm, dbound_hbm,
     enc_out, cross_out,
     q_ref, k_ref, v_ref, gain_ref, gain_c, lens_ref, ebound, dbound,
-    wo, kvw, ctx, hid, hid_c, hid_in, part, x1s, x1r, x2s, x2r, res, acc, sums, out_c, out_in, out_w,
+    wo, kvw, ctx, hid, hid_c, hid_in, part, x1s, x1r, x2s, x2r, res, acc, sums, out_c, out_in, out_w, enc_c,
     ys, yr, st, str_, dq2, dres, drecv,
     in_sem, first_s, first_r, wo_s, wo_r, wof_r, kv_s, kv_r, kvf_r,
     dq_s, dq_r, up_s, up_r, hid_s, hid_r, out_s, out_r, ctx_s, ctx_r, xs1, xr1, xs2, xr2,
@@ -100,8 +100,8 @@
     piece = cols_of(c, PIECE)
     mine = piece
     pairs = (
-        (wk_hbm, kvw.at[0, 0, piece]), (wv_hbm, kvw.at[0, 1, piece]),
-        (hidden, hid.at[:, pl.ds(0, FEAT)]), (hidden, hid.at[:, pl.ds(FEAT, FEAT)]), (wo_hbm, wo.at[mine]),
+        (wo_hbm, wo.at[mine]), (wk_hbm, kvw.at[0, 0, piece]), (wv_hbm, kvw.at[0, 1, piece]),
+        (hidden, hid.at[:, pl.ds(0, FEAT)]), (hidden, hid.at[:, pl.ds(FEAT, FEAT)]),
         (elen_hbm, lens_ref.at[0]), (dlen_hbm, lens_ref.at[1]), (order_hbm, lens_ref.at[2]),
         (ebound_hbm, ebound), (dbound_hbm, dbound),
         (q_hbm, q_ref), (k_hbm, k_ref), (v_hbm, v_ref),
@@ -124,21 +124,21 @@
 
     around = ((z_next, out_at(1)), (cross, in_at(1)), (sib, 0))
     wo_first = [
-        remote(wo_hbm, wo.at[rows_at(to, c * PIECE, PIECE)], wo_s, first_r.at[i], dev)
+        remote(wo.at[mine], wo.at[rows_at(to, c * PIECE, PIECE)], wo_s, first_r.at[i], dev)
         for i, (dev, to) in enumerate(around)
     ]
     kv_first = [
         remote(kvw.at[0, :, piece], kvw.at[to, :, piece], first_s, first_r.at[3 + i], dev)
         for i, (dev, to) in enumerate(around)
     ]
+    loads[0].wait()
     for copy in wo_first:
         copy.start()
-    for load in loads[:2]:
+    for load in loads[1:3]:
         load.wait()
     for copy in kv_first:
         copy.start()
-    dq_copy = remote(dq_hbm, dq2.at[pl.ds(DROWS, DROWS)], dq_s, dq_r, lower)
-    dq_copy.start()
+    dq_copy = remote(dq2.at[pl.ds(0, DROWS)], dq2.at[pl.ds(DROWS, DROWS)], dq_s, dq_r, lower)
 
     def turned(ref, by):
         wider = ref[:, pl.ds(pl.multiple_of((by // 2) * 128, 128), FEAT + 128)].astype(F32)
@@ -156,7 +156,7 @@
     def out_copy(s, r):
         return remote(out_c.at[s, r], out_in.at[s], out_s, out_r.at[s], near[r])
 
-    for load in loads[2:4]:
+    for load in loads[3:5]:
         load.wait()
     hid_turned = turned(hid, z)
     for s in range(STEPS):
@@ -172,7 +172,7 @@
     def _():
         hid_in[:, own] = hid_c[...]
 
-    for load in loads[4:10]:
+    for load in loads[5:10]:
         load.wait()
 
     n = 256
@@ -237,6 +237,7 @@
     forward(1, ring_kv)
     for load in loads[10:]:
         load.wait()
+    dq_copy.start()
     for head in range(2):
         cols = slice(head * HEAD_DIM, (head + 1) * HEAD_DIM)
         ctx[head, own] = attend(q_ref[:, cols], k_ref[:, cols], v_ref[:, cols], enc_allowed)
@@ -392,10 +393,10 @@
     exchange(3, *late, 5)
     pass_on(8, ring_kv)
     fans(1, ring_kv)
-    accumulate(1, *all_rows)
+    accumulate(1, *early)
     finish(2, *all_rows, 3)
     fans(2, ring_kv)
-    accumulate(2, *all_rows)
+    accumulate(2, *early)
     fans(3, ring_kv)
 
     y_copies = [remote(ys.at[i], yr.at[i], y_s, y_r.at[i], (y_a, y_b)[i % 2]) for i in range(6)]
@@ -412,6 +413,8 @@
     y_send(0, acc[0, 0])
     y_send(1, acc[1, 0])
     y_send(2, acc[0, 1])
+    accumulate(1, *late)
+    accumulate(2, *late)
     finish(end, *late, 5)
     accumulate(end, *late)
     y_send(3, acc[1, 2])
@@ -437,7 +440,9 @@
             for copy in range(2):
                 at = slice(cols.start + copy * FEAT, cols.stop + copy * FEAT)
                 out_w[:, at] = out_in[s, half].astype(F32)
-    enc_out[...] = turned(out_w, (NZ - z) % NZ).astype(BF16)
+    enc_c[...] = turned(out_w, (NZ - z) % NZ).astype(BF16)
+    enc_copy = pltpu.make_async_copy(enc_c, enc_out, in_sem.at[0])
+    enc_copy.start()
 
     lower_half = rows_i < DROWS
     above_end = jnp.minimum(w + 2, NW)
@@ -489,6 +494,7 @@
     def _():
         left(out_c.at[pl.ds(0, 3)], out_s)
 
+    enc_copy.wait()
     up.wait()
     cross_out[...] = cross_out[...] + drecv[...]
 
@@ -509,7 +515,7 @@
             jax.ShapeDtypeStruct((DROWS, WID), BF16),
         ),
         in_specs=[anywhere] * 14,
-        out_specs=(vmem, vmem),
+        out_specs=(anywhere, vmem),
         scratch_shapes=[
             pltpu.VMEM((ROWS, WID), BF16),
             pltpu.VMEM((ROWS, WID), BF16),
@@ -536,6 +542,7 @@
             pltpu.VMEM((STEPS, NY, 2) + square, BF16),
             pltpu.VMEM((STEPS, 2) + square, BF16),
             pltpu.VMEM((ROWS, 2 * FEAT), F32),
+            pltpu.VMEM((ROWS, FEAT), BF16),
             pltpu.VMEM((6, ROWS, WID), BF16),
             pltpu.VMEM((6, ROWS, WID), BF16),
             pltpu.VMEM((NY, 8, ROWS), F32),

time: 72.3 us -> 72 us (level)
  no operation moved by 1% of the time
where the time goes in v8:
time: 72 us; the launch traced here: 71.8 us
  Pallas kernels  68.8 us (96%)
  local copies, waits for them, and re-layouts  2.33 us (3%)
    pallas_call x1, Pallas kernels, body(): pl.pallas_call(kernel, out_shape=(jax.ShapeDtypeStruct((ROWS, FEAT), BF16...  68.8 us
    unnamed x4, local copies, waits for them, and re-layouts  2.33 us

profile of v8, /device:TPU:1, one launch (start us, length us, event | category | flops | bytes accessed | tf_op | source)
XLA Modules:
  0.0 71.8 jit_solution(7891872864554733418)
XLA Ops:
  0.6 68.8 %encoder_to_cross.1 = (bf16[128,1024]{1,0:T(8,128)(2,1)}, bf16[64,512]{1,0:T(8,128)(2,1)}) custom-call(bf16[128,1024]{1,0:T(8,128)(2,1)} %hidden.1, bf16[128,512]{1,0:T(8,128)(2,1)} %q_hbm.1, bf16[128,512]{1,0:T(8,128)(2,1)} %k_hbm.1, bf16[128,512]{1,0:T(8,128)(2,1)} %v_hbm.1, bf16[64,512]{1,0:T(8,128)(2,1)} %dq_hbm.1, bf16[32,512]{1,0:T(8,128)(2,1)} %bitcast.5, ...), custom_call_target="tpu_custom_call" | custom-call | tf_op jit(solution)/shard_map/encoder_to_cross/pallas_call | solution.py:511
  69.4 0.0 copy-start
  69.4 1.7 %copy.18 = bf16[128,1024]{1,0:T(8,128)(2,1)} copy(bf16[128,1024]{1,0:T(8,128)(2,1)} %get-tuple-element.4) | data formatting | bytes 524288
  71.1 0.0 copy-done
  71.1 0.6 copy.19
Async XLA Ops:
  69.4 1.7 %copy-start = (bf16[64,512]{1,0:T(8,128)(2,1)S(1)}, bf16[64,512]{1,0:T(8,128)(2,1)}, u32[]{:S(2)}) copy-start(bf16[64,512]{1,0:T(8,128)(2,1)} %get-tuple-element.5) | copy-start | bytes 196612

commit v9 on v8

--- a/solution.py
+++ b/solution.py
@@ -440,7 +440,7 @@
             for copy in range(2):
                 at = slice(cols.start + copy * FEAT, cols.stop + copy * FEAT)
                 out_w[:, at] = out_in[s, half].astype(F32)
-    enc_c[...] = turned(out_w, (NZ - z) % NZ).astype(BF16)
+    enc_c[...] = turned(out_w, (NZ - z) % NZ)
     enc_copy = pltpu.make_async_copy(enc_c, enc_out, in_sem.at[0])
     enc_copy.start()
 
@@ -471,7 +471,7 @@
     dres[...] = jnp.concatenate([cross(slice(DROWS, ROWS), head) for head in range(2)], axis=1)
     up = remote(dres, drecv, up_s, up_r, upper)
     up.start()
-    cross_out[...] = jnp.concatenate([cross(slice(0, DROWS), head) for head in range(2)], axis=1)
+    cross_out[...] = jnp.concatenate([cross(slice(0, DROWS), head) for head in range(2)], axis=1).astype(F32)
 
     def left(sent, sem):
         remote(sent, sent, sem, up_r, sib).wait_send()
@@ -496,7 +496,7 @@
 
     enc_copy.wait()
     up.wait()
-    cross_out[...] = cross_out[...] + drecv[...]
+    cross_out[...] = cross_out[...] + drecv[...].astype(F32)
 
 
 def body(
@@ -508,11 +508,11 @@
     dma = pltpu.SemaphoreType.DMA
     gain = norm_gain.reshape(32, 128)
     square = (ROWS, 128)
-    return pl.pallas_call(
+    hidden, context = pl.pallas_call(
         kernel,
         out_shape=(
-            jax.ShapeDtypeStruct((ROWS, FEAT), BF16),
-            jax.ShapeDtypeStruct((DROWS, WID), BF16),
+            jax.ShapeDtypeStruct((ROWS, FEAT), F32),
+            jax.ShapeDtypeStruct((DROWS, WID), F32),
         ),
         in_specs=[anywhere] * 14,
         out_specs=(anywhere, vmem),
@@ -542,7 +542,7 @@
             pltpu.VMEM((STEPS, NY, 2) + square, BF16),
             pltpu.VMEM((STEPS, 2) + square, BF16),
             pltpu.VMEM((ROWS, 2 * FEAT), F32),
-            pltpu.VMEM((ROWS, FEAT), BF16),
+            pltpu.VMEM((ROWS, FEAT), F32),
             pltpu.VMEM((6, ROWS, WID), BF16),
             pltpu.VMEM((6, ROWS, WID), BF16),
             pltpu.VMEM((NY, 8, ROWS), F32),
@@ -573,6 +573,7 @@
         gain, enc_len.reshape(1, 256), dec_len.reshape(1, 256),
         example_order.reshape(1, 256), enc_bounds, dec_bounds,
     )
+    return hidden.astype(BF16), context.astype(BF16)
 
 
 def solution(mesh):

time: 72 us -> 72.2 us (level)
  other arithmetic: 0 us -> 2.45 us
  local copies, waits for them, and re-layouts: 2.33 us -> 0.01 us
    convert_element_type x0 -> x2, other arithmetic: none -> 2.45 us  [body(): return (hidden.astype(BF16), context.astype(BF16))]
    unnamed x4 -> x2, local copies, waits for them, and re-layouts: 2.33 us -> 0.01 us
where the time goes in v9:
time: 72.2 us; the launch traced here: 71.9 us
  Pallas kernels  68.8 us (95%)
  other arithmetic  2.45 us (3%)
    pallas_call x1, Pallas kernels, body(): pl.pallas_call(kernel, out_shape=(jax.ShapeDtypeStruct((ROWS, FEAT), F32)...  68.8 us
    convert_element_type x2, other arithmetic, body(): return (hidden.astype(BF16), context.astype(BF16))  2.45 us

profile of v9, /device:TPU:1, one launch (start us, length us, event | category | flops | bytes accessed | tf_op | source)
XLA Modules:
  0.0 71.9 jit_solution(5814862261125215791)
XLA Ops:
  0.6 68.8 %encoder_to_cross.1 = (f32[128,1024]{1,0:T(8,128)}, f32[64,512]{1,0:T(8,128)}) custom-call(bf16[128,1024]{1,0:T(8,128)(2,1)} %hidden.1, bf16[128,512]{1,0:T(8,128)(2,1)} %q_hbm.1, bf16[128,512]{1,0:T(8,128)(2,1)} %k_hbm.1, bf16[128,512]{1,0:T(8,128)(2,1)} %v_hbm.1, bf16[64,512]{1,0:T(8,128)(2,1)} %dq_hbm.1, bf16[32,512]{1,0:T(8,128)(2,1)} %bitcast.5, ...), custom_call_target="tpu_custom_call" | custom-call | tf_op jit(solution)/shard_map/encoder_to_cross/pallas_call | solution.py:511
  69.4 0.0 copy-start
  69.4 1.8 %convert_element_type.6 = bf16[128,1024]{1,0:T(8,128)(2,1)} convert(f32[128,1024]{1,0:T(8,128)} %get-tuple-element.4) | non-fusion elementwise | flops 131072 | bytes 786432 | tf_op jit(solution)/shard_map/convert_element_type | solution.py:576
  71.3 0.0 copy-done
  71.3 0.6 convert_element_type.7
Async XLA Ops:
  69.4 1.8 %copy-start = (f32[64,512]{1,0:T(8,128)S(1)}, f32[64,512]{1,0:T(8,128)}, u32[]{:S(2)}) copy-start(f32[64,512]{1,0:T(8,128)} %get-tuple-element.5) | copy-start | bytes 393220

commit v10 on v8

--- a/solution.py
+++ b/solution.py
@@ -388,9 +388,9 @@
     pass_on(7, ring_kv)
     finish(1, *all_rows, 2)
     fans(0, ring_kv)
-    accumulate(0, *all_rows)
     exchange(3, *early, 4)
     exchange(3, *late, 5)
+    accumulate(0, *early)
     pass_on(8, ring_kv)
     fans(1, ring_kv)
     accumulate(1, *early)
@@ -413,6 +413,7 @@
     y_send(0, acc[0, 0])
     y_send(1, acc[1, 0])
     y_send(2, acc[0, 1])
+    accumulate(0, *late)
     accumulate(1, *late)
     accumulate(2, *late)
     finish(end, *late, 5)

time: 72 us -> 72 us (level)
  no operation moved by 1% of the time
where the time goes in v10:
time: 72 us; the launch traced here: 71.8 us
  Pallas kernels  68.8 us (96%)
  local copies, waits for them, and re-layouts  2.33 us (3%)
    pallas_call x1, Pallas kernels, body(): pl.pallas_call(kernel, out_shape=(jax.ShapeDtypeStruct((ROWS, FEAT), BF16...  68.8 us
    unnamed x4, local copies, waits for them, and re-layouts  2.33 us

profile of v10, /device:TPU:1, one launch (start us, length us, event | category | flops | bytes accessed | tf_op | source)
XLA Modules:
  0.0 71.8 jit_solution(14516417709723601547)
XLA Ops:
  0.6 68.8 %encoder_to_cross.1 = (bf16[128,1024]{1,0:T(8,128)(2,1)}, bf16[64,512]{1,0:T(8,128)(2,1)}) custom-call(bf16[128,1024]{1,0:T(8,128)(2,1)} %hidden.1, bf16[128,512]{1,0:T(8,128)(2,1)} %q_hbm.1, bf16[128,512]{1,0:T(8,128)(2,1)} %k_hbm.1, bf16[128,512]{1,0:T(8,128)(2,1)} %v_hbm.1, bf16[64,512]{1,0:T(8,128)(2,1)} %dq_hbm.1, bf16[32,512]{1,0:T(8,128)(2,1)} %bitcast.5, ...), custom_call_target="tpu_custom_call" | custom-call | tf_op jit(solution)/shard_map/encoder_to_cross/pallas_call | solution.py:512
  69.4 0.0 copy-start
  69.4 1.7 %copy.18 = bf16[128,1024]{1,0:T(8,128)(2,1)} copy(bf16[128,1024]{1,0:T(8,128)(2,1)} %get-tuple-element.4) | data formatting | bytes 524288
  71.1 0.0 copy-done
  71.1 0.6 copy.19
Async XLA Ops:
  69.4 1.7 %copy-start = (bf16[64,512]{1,0:T(8,128)(2,1)S(1)}, bf16[64,512]{1,0:T(8,128)(2,1)}, u32[]{:S(2)}) copy-start(bf16[64,512]{1,0:T(8,128)(2,1)} %get-tuple-element.5) | copy-start | bytes 196612
